TPU v7x, 32 devices: a whole 2x2x4 slice. The times are simulated.
32 devices in a mesh: seq: 4 (over y, x), exp: 8 (over z, core).
Axes of the slice: x: 2, y: 2, z: 4, core: 2. Of those that a mesh axis runs over, the one named last changes fastest.
Arguments:
- x_in: bfloat16 [1024, 8192], P('seq', 'exp'), may hold values from -6 to 6
- z_gate: bfloat16 [1024, 8192], P('seq', 'exp'), may hold values from -6 to 6
- b_in: bfloat16 [1024, 128], P('seq'), may hold values from -0.52734375 to 0.52734375
- c_out: bfloat16 [1024, 128], P('seq'), may hold values from -0.375 to 0.375
- dt_step: float32 [1024, 128], P('seq', 'exp'), may hold values from 0.12 to 516, as said below
- rate: float32 [128], P('exp'), may hold values from 0 to 0.06, as said below
- skip: float32 [128], P('exp'), may hold values from 0.5 to 1.5
- init_state: float32 [128, 64, 128], P('exp'), may hold values from -8.485281 to 8.485281
- residual: bfloat16 [1024, 8192], P(('seq', 'exp')), may hold values from -6 to 6
- norm_gain: float32 [8192], replicated, may hold values from 0.5 to 1.5
- expert_ids: int32 [1024, 2], P(('seq', 'exp')), may hold values from 0 to 7, all different within a row; in each aligned block of 32 rows (0 to 31, 32 to 63, ...) at most 9 rows name the same one
- gate_weights: float32 [1024, 2], P(('seq', 'exp')), may hold values from 0.2 to 1
- w_gate: bfloat16 [8, 8192, 2048], P('exp', None, 'seq'), may hold values from -0.0625 to 0.0625
- w_up: bfloat16 [8, 8192, 2048], P('exp', None, 'seq'), may hold values from -0.0625 to 0.0625
- w_down: bfloat16 [8, 2048, 8192], P('exp', 'seq'), may hold values from -0.125 to 0.125
Outputs:
- layer_out: bfloat16 [1024, 8192], P(('seq', 'exp'))
Inputs may be any that keep to these rules, and one draw needn't show every extreme that they name: `dt_step`: positive step sizes. `rate`: positive rates. `expert_ids`: each row names two different experts; among the rows of one device (aligned blocks of 32 rows) no expert is named by more than 9 rows, and in every draw some expert is named by exactly 9 rows of some block.
All inputs are finite; a program needn't handle non-finite values.
Results may differ from a plain program's by a relative error of at most 0.0095.
Values may be sent and summed in bfloat16 or wider, within the bound.
No kernel may reach another device: no remote copies, remote signals or barrier semaphores. Data moves between devices by JAX's collectives and lax.ppermute only.
A program may use at most 128 MiB of HBM per device.

v0:
```python
import functools

import jax
import jax.numpy as jnp
from jax import lax
from jax.experimental import pallas as pl
from jax.experimental.pallas import tpu as pltpu
from jax.sharding import PartitionSpec as P

GROUP = 128
PRECISE = lax.Precision.HIGHEST
F32 = jnp.float32
BF16 = jnp.bfloat16
MIB = 1 << 20
NO_COST = pl.CostEstimate(flops=0, bytes_accessed=0, transcendentals=0)


def block_call(body, outs, scalars, args, held=0, keep=0, after=(), limit=16, out_blocks=False, name=None):
    n_args = len(args)
    kept = [jax.ShapeDtypeStruct(v.shape, v.dtype) for v in args[scalars : scalars + held]]

    def kernel(*refs):
        refs, sems = (refs[:-1], refs[-1]) if held else (refs, None)
        inputs, refs = refs[:n_args], refs[n_args + len(after) :]
        results, refs = refs[: len(outs)], refs[len(outs) :]
        copies = [
            pltpu.make_async_copy(src, dst, sems.at[k])
            for k, (src, dst) in enumerate(zip(inputs[scalars : scalars + held], refs))
        ]
        for copy in copies:
            copy.start()
        for copy in copies:
            copy.wait()
        body(*inputs[:scalars], *refs, *inputs[scalars + held :], *results)

    scratch = [pltpu.VMEM(v.shape, v.dtype) for v in kept[keep:]]
    if held:
        scratch.append(pltpu.SemaphoreType.DMA((held,)))
    return pl.pallas_call(
        kernel,
        name=name or getattr(body, "func", body).__name__,
        out_shape=list(outs) + kept[:keep],
        in_specs=[pl.BlockSpec(memory_space=pltpu.SMEM)] * scalars
        + [pl.BlockSpec(memory_space=pltpu.HBM)] * held
        + [pl.BlockSpec(memory_space=pltpu.VMEM)] * (n_args - scalars - held)
        + [pl.BlockSpec(memory_space=pl.ANY)] * len(after),
        out_specs=[pl.BlockSpec() if out_blocks else pl.BlockSpec(memory_space=pltpu.VMEM)]
        * (len(outs) + keep),
        scratch_shapes=scratch,
        compiler_params=pltpu.CompilerParams(vmem_limit_bytes=limit * MIB),
        cost_estimate=NO_COST,
    )(*args, *after)


def iota(shape, dim):
    return lax.broadcasted_iota(jnp.int32, shape, dim)


def dot(a, b, precision=None):
    return jnp.dot(a, b, precision=precision, preferred_element_type=F32)


def head_spread(heads, channels):
    shape = (heads, channels)
    return (iota(shape, 1) // (channels // heads) == iota(shape, 0)).astype(F32)


def running_logs(dt_t_ref, rate_ref):
    logs = -rate_ref[...] * dt_t_ref[...].T
    tokens = logs.shape[0]
    tri = (iota((tokens, tokens), 0) >= iota((tokens, tokens), 1)).astype(F32)
    return dot(tri, logs, PRECISE)


def pack_kernel(ids_t_ref, residual_ref, out_ref):
    parts, rows, wide = out_ref.shape
    part = wide - 128
    ids = ids_t_ref[...].astype(F32).T
    lane = iota((rows, 128), 1)
    named = jnp.where(lane == 0, ids[:, 0:1], jnp.where(lane == 1, ids[:, 1:2], 0.0)).astype(BF16)
    for k in range(parts):
        out_ref[k, :, 0:part] = residual_ref[:, k * part : (k + 1) * part]
        out_ref[k, :, part:wide] = named


def state_kernel(place, x_ref, b_ref, dt_t_ref, rate_ref, init_ref, payload_ref, init_t_ref):
    tokens, channels = x_ref.shape
    heads = dt_t_ref.shape[0]
    width = b_ref.shape[1]
    cum = running_logs(dt_t_ref, rate_ref)
    total = cum[tokens - 1 : tokens, :]
    spread = head_spread(heads, channels)
    tail = dot(jnp.exp(total - cum), spread, PRECISE)
    scaled = (x_ref[...].astype(F32) * tail).astype(BF16)
    keys = b_ref[...].astype(F32).T.astype(BF16)
    own = dot(keys, scaled)
    decay = dot(jnp.broadcast_to(jnp.exp(total), (8, heads)), spread, PRECISE)
    init_t = init_ref[...].T
    init_t_ref[...] = init_t.astype(BF16)
    first = (place[0] == 0).astype(F32)
    payload_ref[0:width, :] = (own + first * (decay[0:1, :] * init_t)).astype(BF16)
    high = decay.astype(BF16).astype(F32)
    rows = iota((16, channels), 0)
    high16 = jnp.broadcast_to(high[0:1, :], (16, channels))
    low16 = jnp.broadcast_to(decay[0:1, :], (16, channels)) - high16
    payload_ref[width : width + 16, :] = jnp.where(
        rows == 0, high16, jnp.where(rows == 1, low16, 0.0)
    ).astype(BF16)


def intra_kernel(x_ref, z_ref, b_ref, c_ref, dt_t_ref, rate_ref, skip_ref, own_ref, fade_ref, token_ref):
    tokens, channels = x_ref.shape
    heads = dt_t_ref.shape[0]
    width = channels // heads
    token_ref[...] = jnp.zeros_like(token_ref)
    shape = (tokens, tokens)
    causal = iota(shape, 0) >= iota(shape, 1)
    cum = running_logs(dt_t_ref, rate_ref)
    cum_t = cum.T
    scores = lax.dot_general(
        c_ref[...], b_ref[...], (((1,), (1,)), ((), ())), preferred_element_type=F32
    )
    spread = head_spread(heads, channels)
    direct = dot(jnp.broadcast_to(skip_ref[...], (8, heads)), spread, PRECISE)[0:1, :]
    fade = dot(jnp.exp(cum), spread, PRECISE)
    per = 128 // width
    lane_head = iota((tokens, 128), 1) // width
    for group in range(heads // per):
        cols = slice(group * 128, (group + 1) * 128)
        x = x_ref[:, cols]
        total = x.astype(F32) * direct[:, cols]
        for k in range(per):
            h = group * per + k
            gap = jnp.where(causal, cum[:, h : h + 1] - cum_t[h : h + 1, :], -1e30)
            weights = (jnp.exp(gap) * scores).astype(BF16)
            part = dot(weights, x)
            total = total + jnp.where(lane_head == k, part, 0.0)
        z = z_ref[:, cols].astype(F32)
        gate = z / (1.0 + jnp.exp(-z))
        own_ref[:, cols] = total * gate
        fade_ref[:, cols] = fade[:, cols] * gate


def place_kernel(cap, experts, me, packed_ref, *refs):
    count = (len(refs) - 1) // 2
    out_ref = refs[count]
    for source, target in zip(refs[:count], refs[count + 1 :]):
        target[...] = source[...]
    blocks, rows, wide = packed_ref.shape
    tokens = blocks * rows
    slots = out_ref.shape[1] - rows
    ids = packed_ref[:, :, wide - 128 : wide].astype(F32).reshape(tokens, 128).T
    ids = ids[0:8, :].astype(jnp.int32)
    shape = (tokens, tokens)
    before = (iota(shape, 0) < iota(shape, 1)) & (iota(shape, 0) // rows == iota(shape, 1) // rows)
    named = iota((experts, tokens), 0) ^ me[0]
    hit = (ids[0:1, :] == named) | (ids[1:2, :] == named)
    rank = dot(hit.astype(BF16), before.astype(BF16)).astype(jnp.int32)
    block = (iota((experts, tokens), 1) // rows) ^ named
    whole = cap - 1
    row = jnp.where(rank < whole, block * whole + rank, blocks * whole + block)
    row = jnp.where(hit, row, -1)
    shape = (rows + slots, tokens)
    for e in range(experts):
        owned = ((me[0] ^ e) * rows + iota(shape, 0) == iota(shape, 1)) & (iota(shape, 0) < rows)
        placed = (iota(shape, 0) - rows == row[e : e + 1, :]) & (iota(shape, 0) >= rows)
        out_ref[e] = (owned | placed).astype(F32).astype(BF16)


def join_kernel(place, own_ref, other_ref, out_ref):
    width = out_ref.shape[0]
    odd = place[0] % 2 == 1
    own, other = own_ref[0:width, :].astype(F32), other_ref[0:width, :].astype(F32)
    own_decay = own_ref[width : width + 16, :].astype(F32)
    other_decay = other_ref[width : width + 16, :].astype(F32)
    own_decay = own_decay[0:1, :] + own_decay[1:2, :]
    other_decay = other_decay[0:1, :] + other_decay[1:2, :]
    early = jnp.where(odd, other, own)
    late = jnp.where(odd, own, other)
    decay = jnp.where(odd, own_decay, other_decay)
    out_ref[...] = (decay * early + late).astype(BF16)


def stream_kernel(
    place, c_ref, own_ref, fade_ref, init_t_ref, pair_ref, early_ref, res_ref, sel_ref, same_ref, other_ref
):
    width = init_t_ref.shape[0]
    at = place[0]
    zero = (at == 0).astype(F32)
    odd = (at % 2 == 1).astype(F32)
    pair = pair_ref[...].astype(F32)
    decay = pair[width : width + 1, :] + pair[width + 1 : width + 2, :]
    factor = jnp.where(at >= 2, jnp.where(at % 2 == 1, decay, 1.0), 0.0)
    entering = zero * init_t_ref[...].astype(F32) + odd * pair[0:width, :] + factor * early_ref[...].astype(F32)
    mixed = own_ref[...] + fade_ref[...] * dot(c_ref[...], entering.astype(BF16))
    mixer = mixed.astype(BF16).astype(F32)
    tokens, channels = mixer.shape
    residual = res_ref[:, :, 0:channels].astype(F32).reshape(tokens, channels)
    stream = (residual + mixer).astype(BF16)
    for k in range(same_ref.shape[0]):
        same_ref[k] = dot(sel_ref[2 * k], stream).astype(BF16)
        other_ref[k] = dot(sel_ref[2 * k + 1], stream).astype(BF16)


def up_kernel(first, features, after, me, *refs):
    own, rx, ry, even, odd, gain, wg, wu = refs[:8]
    carry = () if first else refs[8:11]
    rest = refs[(8 if first else 11) + after :]
    sums = rest[2:5] if features else rest
    step = pl.program_id(0)
    steps = pl.num_programs(0)

    if first or features:

        @pl.when(step == 0)
        def _():
            for i, acc in enumerate(sums):
                acc[...] = jnp.zeros_like(acc) if first else carry[i][...]

    gate, up, square = sums
    slots = own.shape[1]
    rows = [r[0].astype(F32) for r in (own, rx, ry)]
    rows.append(jnp.where(step == 0, even[0].astype(F32), odd[0].astype(F32)))
    rows = jnp.concatenate(rows, axis=0)
    square[...] += jnp.broadcast_to(jnp.sum(rows * rows, axis=1, keepdims=True), square.shape)
    scaled = (rows * gain[0]).astype(BF16)
    gate[...] += dot(scaled, wg[0])
    up[...] += dot(scaled, wu[0])

    if features:
        outs, stages = rest[:2], rest[5:]

        @pl.when(step == steps - 1)
        def _():
            inverse = lax.rsqrt(square[:, 0:1] * (1.0 / features) + 1e-06)
            g = gate[...] * inverse
            active = g / (1.0 + jnp.exp(-g)) * (up[...] * inverse)
            main, ninths = slots // 9 * 8, slots // 9
            for d in range(4):
                at = d * slots
                stage, d, shards = (stages[0], 0, 1) if d == 3 else (stages[1], d, 3)
                stage[d * main : (d + 1) * main, :] = active[at : at + main]
                low = shards * main + d * ninths
                stage[low : low + ninths, :] = active[at + main : at + slots]
            for out, stage in zip(outs, stages):
                out[...] = stage[...].astype(BF16)


def up_project(group, last, me, near, far, gain, w_gate, w_up, carry, after=()):
    slots, part = near[0][0].shape[1:]
    hidden = w_gate.shape[2]
    total = 4 * slots
    source = lambda i, me: me[0] ^ (2 * group + i)
    rows = [
        pl.BlockSpec((1, slots, part), lambda i, me, start=start: (start + i, 0, 0))
        for _, start in near
    ] + [
        pl.BlockSpec((1, slots, part), lambda i, me, start=start: (start, 0, 0)) for _, start in far
    ]
    weight = pl.BlockSpec((1, part, hidden), lambda i, me: (source(i, me), 0, 0))
    in_place = pl.BlockSpec(memory_space=pltpu.VMEM)
    specs = rows + [pl.BlockSpec((1, 1, part), lambda i, me: (source(i, me), 0, 0)), weight, weight]
    sums = [
        jax.ShapeDtypeStruct((total, hidden), F32),
        jax.ShapeDtypeStruct((total, hidden), F32),
        jax.ShapeDtypeStruct((total, 128), F32),
    ]
    aliases = {}
    if carry is not None:
        specs += [in_place] * 3
        if not last:
            aliases = {9 + i: i for i in range(3)}
    specs += [pl.BlockSpec(memory_space=pl.ANY)] * len(after)
    sizes = (slots, 3 * slots)
    outs = [jax.ShapeDtypeStruct((n, hidden), BF16) for n in sizes] if last else sums
    scratch = [pltpu.VMEM(s.shape, s.dtype) for s in sums]
    scratch += [pltpu.VMEM((n, hidden), F32) for n in sizes]
    features = gain.shape[0] * part if last else 0
    return pl.pallas_call(
        functools.partial(up_kernel, carry is None, features, len(after)),
        name=f"up_{group}",
        out_shape=outs,
        grid_spec=pltpu.PrefetchScalarGridSpec(
            num_scalar_prefetch=1,
            grid=(2,),
            in_specs=specs,
            out_specs=[in_place] * len(outs),
            scratch_shapes=scratch if last else [],
        ),
        input_output_aliases=aliases,
        compiler_params=pltpu.CompilerParams(vmem_limit_bytes=48 * MIB),
        cost_estimate=NO_COST,
    )(me, *(array for array, _ in near + far), gain, w_gate, w_up, *(carry or ()), *after)


def cut_of(group):
    return 5 if group % 2 else 4


def down_kernel(groups, act_ref, w_ref, *refs):
    outs, spare = refs[:-1], refs[-1]
    step = pl.program_id(0)
    part = dot(act_ref[...], w_ref[...])
    ninths = part.shape[0] // 9
    main = part.shape[0] - ninths
    shards = ninths // (2 * groups)

    def through(group, tile):
        to_x, to_y = outs[2 * (group // 2) : 2 * (group // 2) + 2]
        cut = cut_of(group)
        return to_x, tile + (0 if group % 2 else 5), to_y, tile - cut + (0 if group % 2 else 4)

    for shard in range(shards):
        for group in range(groups):
            at = (shard * groups + group) * 16
            rows = part[at : at + 16, :].astype(BF16)
            if shards > 1:
                outs[shards * group + shard][step] = rows
                continue
            to_x, place_x, to_y, place_y = through(group, step)

            @pl.when(step < cut_of(group))
            def _():
                to_x[place_x] = rows

            @pl.when(step >= cut_of(group))
            def _():
                to_y[place_y] = rows

    for lanes in range(spare.shape[0]):
        spare[lanes, pl.ds(pl.multiple_of(step * ninths, 8), ninths), :] = part[
            main:, lanes * 128 : (lanes + 1) * 128
        ]

    @pl.when(step == pl.num_programs(0) - 1)
    def _():
        for shard in range(shards):
            for group in range(groups):
                pair = []
                for side in range(2):
                    row = pl.ds((shard * groups + group) * 2 + side, 8, stride=ninths)
                    ninth = [spare[lanes, row, :] for lanes in range(spare.shape[0])]
                    pair.append(jnp.concatenate(ninth, axis=1))
                pair = jnp.concatenate(pair, axis=0).astype(BF16)
                if shards > 1:
                    outs[shards * group + shard][8] = pair
                else:
                    _, _, to_y, place_y = through(group, 8)
                    to_y[place_y] = pair


def down_project(name, groups, active, w_down):
    total, hidden = active.shape
    features = w_down.shape[1]
    tile = features // 8
    outs = [jax.ShapeDtypeStruct((9, 16, tile), BF16)] * (total // 18)
    return pl.pallas_call(
        functools.partial(down_kernel, groups),
        name=name,
        grid=(8,),
        out_shape=outs,
        in_specs=[
            pl.BlockSpec(memory_space=pltpu.VMEM),
            pl.BlockSpec((hidden, tile), lambda i: (0, i)),
        ],
        out_specs=[pl.BlockSpec(memory_space=pltpu.VMEM)] * len(outs),
        scratch_shapes=[pltpu.VMEM((tile // 128, 8 * total // 9, 128), F32)],
        compiler_params=pltpu.CompilerParams(vmem_limit_bytes=48 * MIB),
        cost_estimate=NO_COST,
    )(active, w_down)


def pair_kernel(same, other, *outs):
    groups = len(outs) // 2
    owned = outs[groups].shape[1]
    for k in range(groups):
        for side, rows in enumerate((same, other)):
            outs[k][side] = rows[k, owned:, :]
            outs[groups + k][side] = rows[k, 0:owned, :]


def second_kernel(*refs):
    parts, out = refs[:-1], refs[-1]
    for h in range(out.shape[0]):
        for k in range(out.shape[1]):
            pair = [ref[k].astype(F32)[8:16] for ref in parts[2 * h : 2 * h + 2]]
            out[h, k] = jnp.concatenate(pair, axis=0).astype(BF16)


def holds_kernel(*refs):
    for source, target in zip(refs[: len(refs) // 2], refs[len(refs) // 2 :]):
        target[...] = source[...]


def hold_kernel(a, out):
    out[...] = a[...]


def half_message_kernel(rx, ry, out_x, out_y):
    out_x[0], out_y[0] = ry[1], rx[0]


def join_message_kernel(own, rx, ry, out_x, out_y):
    out_x[0:2], out_y[0:2] = own[...], own[...]
    out_x[2], out_y[2] = ry[1], rx[0]


def relay_kernel(through_x, through_y, *refs):
    ahead = refs[4 : 4 + (len(refs) - 8) // 2]
    outs, copies = refs[4 + len(ahead) :][:4], refs[8 + len(ahead) :]
    for group in range(2):
        cut = cut_of(group)
        at_x, at_y = (0, -cut) if group else (5, 0)
        for own, out, through, tiles, at in (
            (refs[2 * group], outs[2 * group], through_y, range(cut, 9), at_y),
            (refs[2 * group + 1], outs[2 * group + 1], through_x, range(cut), at_x),
        ):
            for k in range(9):
                if k in tiles:
                    out[k] = (own[k].astype(F32) + through[k + at].astype(F32)).astype(BF16)
                else:
                    out[k] = own[k]
    for source, copy in zip(ahead, copies):
        copy[...] = source[...]


def finish_kernel(own, rx, ry, *refs):
    ahead = refs[: (len(refs) - 1) // 2]
    out, copies = refs[len(ahead)], refs[len(ahead) + 1 :]
    for k in range(9):
        out[k] = (own[k].astype(F32) + rx[k].astype(F32) + ry[k].astype(F32)).astype(BF16)
    for source, copy in zip(ahead, copies):
        copy[...] = source[...]


def mix_kernel(me, ids_t_ref, weight_t_ref, swap_ref, *refs):
    groups = (len(refs) - 1) // 2
    firsts, streams, out_ref = refs[:groups], refs[groups:-1], refs[-1]
    rows = ids_t_ref.shape[1]
    experts = 2 * groups
    pieces = firsts[0].shape[0] - 1
    tile = firsts[0].shape[2]
    ids, weights = ids_t_ref[...].T, weight_t_ref[...].T
    named = iota((rows, experts), 1) ^ me[0]
    first, second = ids[:, 0:1] == named, ids[:, 1:2] == named
    weight = jnp.where(first, weights[:, 0:1], jnp.where(second, weights[:, 1:2], 0.0))
    hit = (first | second).astype(F32)
    before = (iota((rows, rows), 0) > iota((rows, rows), 1)).astype(F32)
    rank = dot(before, hit)
    lanes = 2 * experts * 8
    shape = (experts, lanes)
    spread = ((iota(shape, 1) // 8) % experts == iota(shape, 0)).astype(F32)
    weight = dot(weight, spread, PRECISE)
    rank = dot(rank, spread, PRECISE).astype(jnp.int32)
    lane = iota((rows, lanes), 1)
    main = (lane < experts * 8) & (rank == lane % 8)
    extra = (lane >= experts * 8) & (rank == 8)

    def rows_of(k):
        data = []
        for g in range(groups):
            data.append(firsts[g][k].astype(F32)[0:8])
            data.append(swap_ref[g // 2, k].astype(F32)[g % 2 * 8 : g % 2 * 8 + 8])
        return data

    last = rows_of(pieces)
    for m in range(experts):
        k = me[0] ^ m
        coef = jnp.where(main | (extra & (lane % 8 == k)), weight, 0.0)
        high = coef.astype(BF16)
        low = (coef - high.astype(F32)).astype(BF16)
        data = jnp.concatenate(rows_of(k) + last, axis=0).astype(BF16)
        stream = streams[m // 2][m % 2].astype(F32)
        out_ref[:, pl.ds(pl.multiple_of(k * tile, 128), tile)] = (
            stream + (dot(high, data) + dot(low, data))
        ).astype(BF16)


def on_square(
    x_in,
    z_gate,
    b_in,
    c_out,
    dt_step,
    rate,
    skip,
    init_state,
    residual,
    norm_gain,
    expert_ids,
    gate_weights,
    w_gate,
    w_up,
    w_down,
):
    tokens, channels = x_in.shape
    heads = rate.shape[0]
    state = b_in.shape[1]
    owners = lax.axis_size("exp")
    rows, features = residual.shape
    experts = owners
    cap = max(2, 2 * rows // experts + 1)
    slots = owners * cap
    at = lax.axis_index("seq")
    me = lax.axis_index("exp")
    place = jnp.reshape(at, (1,)).astype(jnp.int32)
    self_id = jnp.reshape(me, (1,)).astype(jnp.int32)

    def over_x(v):
        return lax.ppermute(v, "seq", [(i, i ^ 1) for i in range(4)])

    def over_y(v):
        return lax.ppermute(v, "seq", [(i, i ^ 2) for i in range(4)])

    def along(v, mask):
        return lax.ppermute(v, "exp", [(i, i ^ mask) for i in range(owners)])

    rate_row = rate[None, :]
    dt_t = dt_step.T
    ids_t = expert_ids.T
    packed = block_call(
        pack_kernel,
        [jax.ShapeDtypeStruct((owners, rows, channels + 128), BF16)],
        0,
        (ids_t, residual),
        held=2,
        limit=48,
    )[0]
    packed = lax.all_to_all(packed, "exp", split_axis=0, concat_axis=0, tiled=True)
    payload, init_t = block_call(
        state_kernel,
        [
            jax.ShapeDtypeStruct((state + 16, channels), BF16),
            jax.ShapeDtypeStruct((state, channels), BF16),
        ],
        1,
        (place, x_in, b_in, dt_t, rate_row, init_state.reshape(channels, state)),
        held=5,
        limit=62,
    )
    pair = over_x(payload)
    own_part, fade, token = block_call(
        intra_kernel,
        [
            jax.ShapeDtypeStruct((tokens, channels), F32),
            jax.ShapeDtypeStruct((tokens, channels), F32),
            jax.ShapeDtypeStruct((8, 128), F32),
        ],
        0,
        (x_in, z_gate, b_in, c_out, dt_t, rate_row, skip[None, :]),
        held=7,
        limit=61,
    )
    joined = block_call(
        join_kernel,
        [jax.ShapeDtypeStruct((state, channels), BF16)],
        1,
        (place, payload, pair),
        after=(token,),
    )[0]
    early = over_y(joined)
    handed = (own_part, fade, c_out, init_t)
    select, own_part, fade, c, init_t = block_call(
        functools.partial(place_kernel, cap, experts),
        [jax.ShapeDtypeStruct((experts, rows + slots, tokens), BF16)]
        + [jax.ShapeDtypeStruct(v.shape, v.dtype) for v in handed],
        1,
        (self_id, packed, *handed),
        after=(joined,),
    )
    groups = owners // 2
    lanes = jax.ShapeDtypeStruct((groups, rows + slots, channels), BF16)
    same, other = block_call(
        stream_kernel,
        [lanes, lanes],
        1,
        (place, c, own_part, fade, init_t, pair, early, packed, select),
    )

    gain = norm_gain.reshape(owners, 1, channels)
    wg = w_gate.reshape(owners, channels, w_gate.shape[2])
    wu = w_up.reshape(owners, channels, w_up.shape[2])
    sets = list(block_call(
        pair_kernel,
        [jax.ShapeDtypeStruct((2, slots, channels), BF16)] * groups
        + [jax.ShapeDtypeStruct((2, rows, channels), BF16)] * groups,
        0,
        (same, along(other, 1)),
    ))
    sets, streams = sets[:groups], sets[groups:]
    def hold(v, after, name):
        return block_call(
            hold_kernel, [jax.ShapeDtypeStruct(v.shape, BF16)], 0, (v,), after=after, name=name
        )[0]

    def project(group, near, far, carry, after=()):
        last = group == groups - 1
        return up_project(group, last, self_id, near, far, gain, wg, wu, carry, after)

    def message(count):
        return [jax.ShapeDtypeStruct((count,) + sets[0].shape[1:], BF16)] * 2

    near, far, farthest = along(sets[1], 2), along(sets[2], 4), sets[3]
    rx0, ry0 = over_x(sets[0]), over_y(sets[0])
    to_x, to_y = block_call(half_message_kernel, message(1), 0, (rx0, ry0), name="half_0")
    fx0, fy0 = over_x(to_x), over_y(to_y)
    near = hold(near, (to_x,), "hold_near")
    farthest_held = hold(farthest, (far,), "hold_farthest")
    farthest = along(farthest_held, 6)
    rx1, ry1 = over_x(near), over_y(near)
    to_x, to_y = block_call(
        join_message_kernel, message(3), 0, (far, rx1, ry1), after=(fx0, fy0, farthest_held), name="join_2"
    )
    rx2, ry2 = over_x(to_x), over_y(to_y)
    carry = project(
        0, [(sets[0], 0), (rx0, 0), (ry0, 0)], [(fy0, 0), (fx0, 0)], None
    )
    to_x, to_y = block_call(
        join_message_kernel, message(3), 0, (farthest, rx2, ry2), after=(carry[2],), name="join_3"
    )
    rx3, ry3 = over_x(to_x), over_y(to_y)
    carry = project(1, [(near, 0), (rx1, 0), (ry1, 0)], [(ry2, 2), (rx2, 2)], carry)
    to_x, to_y = block_call(
        half_message_kernel, message(1), 0, (rx3, ry3), after=(carry[2],), name="half_3"
    )
    fx3, fy3 = over_x(to_x), over_y(to_y)
    held = block_call(
        holds_kernel,
        [jax.ShapeDtypeStruct(v.shape, BF16) for v in streams[1:]],
        0,
        streams[1:],
        after=(to_x,),
        name="hold_streams",
    )
    streams[1:] = [along(held[g - 1], 2 * g) for g in range(1, groups)]
    carry = project(2, [(far, 0), (rx2, 0), (ry2, 0)], [(ry3, 2), (rx3, 2)], carry, held[:1])
    active_far, active = project(
        3, [(farthest, 0), (rx3, 0), (ry3, 0)], [(fy3, 0), (fx3, 0)], carry
    )

    wd = w_down.reshape(w_down.shape[1], features)
    tiles = jax.ShapeDtypeStruct((9, 16, features // 8), BF16)
    sent = down_project("down_through", groups, active_far, wd)
    rest = down_project("down_rest", groups, active, wd)
    own, own_x, own_y = ([rest[3 * g + k] for g in range(groups)] for k in range(3))

    def relay(name, through_x, through_y, low, ahead=(), after=()):
        shares = (own_x[low], own_y[low], own_x[low + 1], own_y[low + 1])
        return block_call(
            relay_kernel,
            [tiles] * (4 + len(ahead)),
            0,
            (through_x, through_y, *shares, *ahead),
            after=after,
            name=name,
        )

    def finish(group, rx, ry, ahead=(), after=()):
        return block_call(
            finish_kernel,
            [tiles] * (1 + len(ahead)),
            0,
            (own[group], rx, ry, *ahead),
            after=after,
            name=f"finish_{group}",
        )

    through_x, through_y = over_x(sent[2]), over_y(sent[3])
    x2, y2, x3, y3, next_x, next_y = relay(
        "relay_far", through_x, through_y, 2, (sent[0], sent[1]), streams[1:]
    )
    rx3, ry3 = over_x(x3), over_y(y3)
    through_x, through_y = over_x(next_x), over_y(next_y)
    both3, x2, y2 = finish(3, rx3, ry3, (x2, y2))
    back3 = along(both3, 6)
    rx2, ry2 = over_x(x2), over_y(y2)
    x0, y0, x1, y1 = relay("relay_near", through_x, through_y, 0, after=(both3,))
    rx1, ry1 = over_x(x1), over_y(y1)
    both2, x0, y0 = finish(2, rx2, ry2, (x0, y0))
    back2 = along(both2, 4)
    rx0, ry0 = over_x(x0), over_y(y0)
    back1 = along(finish(1, rx1, ry1, after=(back3,))[0], 2)
    back = [finish(0, rx0, ry0)[0], back1, back2, back3]
    swap = block_call(second_kernel, [jax.ShapeDtypeStruct((2,) + tiles.shape, BF16)], 0, back)[0]
    swap = along(swap, 1)
    return block_call(
        mix_kernel,
        [jax.ShapeDtypeStruct((rows, features), BF16)],
        1,
        (self_id, ids_t, gate_weights.T, swap, *back, *streams),
    )[0]


def entering_2(array, axis, combine, identity):
    devices, mine = (lax.axis_size(axis), lax.axis_index(axis))
    everything = jax.tree.map(
        lambda part, kind: lax.all_gather(part.astype(kind), axis),
        array,
        (jnp.bfloat16, jnp.bfloat16),
    )
    start = jax.tree.map(
        lambda part, zero: jnp.broadcast_to(jnp.asarray(zero, part.dtype), part.shape),
        array,
        identity,
    )

    def hop(k, before):
        reached = k < mine
        new = combine(
            before, jax.tree.map(lambda part, own: part[k].astype(own.dtype), everything, array)
        )
        return jax.tree.map(lambda a, b: jnp.where(reached, a, b), new, before)

    return lax.fori_loop(0, devices, hop, start)


def chain_combine(earlier, later):
    return (earlier[0] + later[0], jnp.exp(later[0])[:, None, None] * earlier[1] + later[1])


def on_device(
    x_in,
    z_gate,
    b_in,
    c_out,
    dt_step,
    rate,
    skip,
    init_state,
    residual,
    norm_gain,
    expert_ids,
    gate_weights,
    w_gate,
    w_up,
    w_down,
):
    token_count, channels = x_in.shape
    heads_here = rate.shape[0]
    head_width = channels // heads_here
    state_width = b_in.shape[1]
    blocks = token_count // GROUP
    inputs = x_in.astype(jnp.float32).reshape(blocks, GROUP, heads_here, head_width)
    keys_in = b_in.astype(jnp.float32).reshape(blocks, GROUP, state_width)
    queries = c_out.astype(jnp.float32).reshape(blocks, GROUP, state_width)
    log_steps = (-rate[None, :] * dt_step).reshape(blocks, GROUP, heads_here)
    cumulative = jnp.cumsum(log_steps, axis=1)
    scores = jnp.einsum("ctn,csn->cts", queries, keys_in, precision=PRECISE)
    causal = jnp.arange(GROUP)[:, None] >= jnp.arange(GROUP)[None, :]
    spread = cumulative[:, :, None, :] - cumulative[:, None, :, :]
    weights = jnp.exp(jnp.where(causal[None, :, :, None], spread, -jnp.inf)) * scores[..., None]
    intra_out = jnp.einsum("ctsh,cshp->cthp", weights, inputs, precision=PRECISE)
    tail_decay = jnp.exp(cumulative[:, -1:, :] - cumulative)
    block_state = jnp.einsum("csh,cshp,csn->chpn", tail_decay, inputs, keys_in, precision=PRECISE)
    block_log = cumulative[:, -1, :]

    def advance(carried, element):
        total_log, total_state = carried
        step_log, step_state = element
        updated = (
            total_log + step_log,
            jnp.exp(step_log)[:, None, None] * total_state + step_state,
        )
        return (updated, (total_log, total_state))

    zero_state = jnp.zeros((heads_here, head_width, state_width), jnp.float32)
    zero_log = jnp.zeros((heads_here,), jnp.float32)
    (device_log, device_state), (enter_log, enter_state) = lax.scan(
        advance, (zero_log, zero_state), (block_log, block_state)
    )
    prior_log, prior_state = entering_2(
        (device_log, device_state), "seq", chain_combine, (zero_log, zero_state)
    )
    incoming = prior_state + jnp.exp(prior_log)[:, None, None] * init_state
    entering = enter_state + jnp.exp(enter_log)[:, :, None, None] * incoming[None]
    inter_out = jnp.exp(cumulative)[..., None] * jnp.einsum(
        "chpn,ctn->cthp", entering, queries, precision=PRECISE
    )
    mixed_out = (intra_out + inter_out + skip[None, None, :, None] * inputs).reshape(
        token_count, channels
    )
    mixer = (mixed_out * jax.nn.silu(z_gate.astype(jnp.float32))).astype(jnp.bfloat16)
    token_mix = lax.all_to_all(mixer, "exp", split_axis=0, concat_axis=1, tiled=True)
    stream = (residual.astype(jnp.float32) + token_mix.astype(jnp.float32)).astype(jnp.bfloat16)
    widened = stream.astype(jnp.float32)
    normed = (
        widened
        * lax.rsqrt(jnp.mean(widened * widened, axis=-1, keepdims=True) + 1e-06)
        * norm_gain[None, :]
    ).astype(jnp.bfloat16)
    rows_here = residual.shape[0]
    owners = lax.axis_size("exp")
    local_experts = w_gate.shape[0]
    experts = owners * local_experts
    capacity = max(2, 2 * rows_here // experts + 1)
    width = residual.shape[1]
    chosen = expert_ids.reshape(-1)
    onehot = (chosen[:, None] == jnp.arange(experts)[None, :]).astype(jnp.int32)
    slot_index = jnp.sum((jnp.cumsum(onehot, axis=0) - onehot) * onehot, axis=1)
    target = chosen * capacity + slot_index
    placing = (target[None, :] == jnp.arange(experts * capacity)[:, None]).astype(jnp.bfloat16)
    pair_rows = jnp.repeat(normed, 2, axis=0)
    outgoing = jnp.dot(placing, pair_rows, preferred_element_type=jnp.float32).astype(jnp.bfloat16)
    outgoing = outgoing.reshape(owners, local_experts, 1, capacity, width)
    arrived = lax.all_to_all(outgoing, "exp", split_axis=0, concat_axis=2, tiled=True)
    segment = lax.all_gather(arrived, "seq", axis=1, tiled=True)
    flattened = segment.reshape(segment.shape[0], -1, segment.shape[-1])
    gate_proj = jnp.einsum("erd,edf->erf", flattened, w_gate, preferred_element_type=jnp.float32)
    up_proj = jnp.einsum("erd,edf->erf", flattened, w_up, preferred_element_type=jnp.float32)
    active = (jax.nn.silu(gate_proj) * up_proj).astype(jnp.bfloat16)
    partial_value = jnp.einsum("erf,efd->erd", active, w_down, preferred_element_type=jnp.float32)
    partials = partial_value.reshape(segment.shape[:-1] + (partial_value.shape[-1],))
    summed = lax.psum_scatter(partials.astype(jnp.bfloat16), "seq", scatter_dimension=1, tiled=True)
    returned = lax.all_to_all(summed, "exp", split_axis=2, concat_axis=0, tiled=True)
    results = returned.reshape(experts * capacity, width)
    picked = results[target].astype(jnp.float32).reshape(rows_here, 2, width)
    mixture = jnp.sum(picked * gate_weights[:, :, None], axis=1)
    return (widened + mixture).astype(jnp.bfloat16)


def solution(mesh):
    square = mesh.shape["seq"] == 4 and mesh.shape["exp"] == 8

    def body(*args):
        rows = args[8].shape[0]
        experts = mesh.shape["exp"] * args[12].shape[0]
        fits = args[12].shape[0] == 1 and 2 * rows // experts + 1 == 9
        return (on_square if square and fits else on_device)(*args)

    return jax.shard_map(
        body,
        mesh=mesh,
        in_specs=(
            P("seq", "exp"),
            P("seq", "exp"),
            P("seq", None),
            P("seq", None),
            P("seq", "exp"),
            P("exp"),
            P("exp"),
            P("exp", None, None),
            P(("seq", "exp"), None),
            P(),
            P(("seq", "exp"), None),
            P(("seq", "exp"), None),
            P("exp", None, "seq"),
            P("exp", None, "seq"),
            P("exp", "seq", None),
        ),
        out_specs=P(("seq", "exp"), None),
        check_vma=False,
    )
```

profile of v0, /device:TPU:0, one launch (start us, length us, event | category | flops | bytes accessed | tf_op | source)
XLA Modules:
  0.0 157.3 jit_solution(13622982161268099804)
XLA Ops:
  0.0 1.0 copy-done.3
  1.0 0.7 copy-done.8
  1.7 1.0 pack_kernel.1
  2.8 6.3 %all-to-all-start = ((bf16[8,32,1152]{2,1,0:T(8,128)(2,1)}), bf16[8,32,1152]{2,1,0:T(8,128)(2,1)S(1)}, u32[]{:S(2)}, u32[]{:S(2)}) async-start(bf16[8,32,1152]{2,1,0:T(8,128)(2,1)} %pack_kernel.1), calls=%async_computation | async-start | bytes 1179648 | tf_op jit(solution)/shard_map/all_to_all | solution.py:529
  9.1 4.1 %state_kernel.1 = (bf16[144,1024]{1,0:T(8,128)(2,1)}, bf16[128,1024]{1,0:T(8,128)(2,1)}) custom-call(s32[1]{0:T(128)} %bitcast.3.refs_0_, bf16[256,1024]{1,0:T(8,128)(2,1)} %refs_1_.5, bf16[256,128]{1,0:T(8,128)(2,1)} %refs_2_.3, f32[16,256]{1,0:T(8,128)} %bitcast.30, f32[1,16]{1,0:T(1,128)} %bitcast.32, f32[1024,128]{1,0:T(8,128)} %bitcast.29), custom_call_target="tpu_custom_call" | custom-call | tf_op jit(solution)/shard_map/state_kernel/pallas_call | solution.py:39
  13.2 1.6 collective-permute-start
  14.8 4.7 %intra_kernel.1 = (f32[256,1024]{1,0:T(8,128)}, f32[256,1024]{1,0:T(8,128)}, f32[8,128]{1,0:T(8,128)}) custom-call(bf16[256,1024]{1,0:T(8,128)(2,1)} %refs_1_.5, bf16[256,1024]{1,0:T(8,128)(2,1)} %refs_1_.4, bf16[256,128]{1,0:T(8,128)(2,1)} %refs_2_.3, bf16[256,128]{1,0:T(8,128)(2,1)} %refs_4_.1, f32[16,256]{1,0:T(8,128)} %bitcast.31, f32[1,16]{1,0:T(1,128)} %bitcast.33, ...), custom_call_target="tpu_custom_call" | custom-call | tf_op jit(solution)/shard_map/intra_kernel/pallas_call | solution.py:39
  19.5 3.4 %collective-permute-done.refs_2_.refs_5_ = bf16[144,1024]{1,0:T(8,128)(2,1)S(1)} collective-permute-done((bf16[144,1024]{1,0:T(8,128)(2,1)}, bf16[144,1024]{1,0:T(8,128)(2,1)S(1)}, u32[]{:S(2)}, u32[]{:S(2)}) %collective-permute-start) | collective-permute-done | bytes 294944 | tf_op jit(solution)/shard_map/ppermute | solution.py:510
  22.9 1.0 copy-done.4
  23.9 0.7 copy-done.7
  24.7 1.6 %collective-permute-start.1 = (bf16[128,1024]{1,0:T(8,128)(2,1)S(1)}, bf16[128,1024]{1,0:T(8,128)(2,1)S(1)}, u32[]{:S(2)}, u32[]{:S(2)}) collective-permute-start(bf16[128,1024]{1,0:T(8,128)(2,1)S(1)} %join_kernel.1.refs_6_), channel_id=1, source_target_pairs={{0,16},{8,24},{16,0},{24,8},{1,17},{9,25},{17,1},{25,9},{2,18},{10... | collective-permute-start | bytes 786440 | tf_op jit(solution)/shard_map/ppermute | solution.py:513
  26.3 1.2 copy-done
  27.5 1.2 copy-done.1
  28.7 0.9 copy-done.5
  29.7 0.8 copy-done.6
  30.9 1.8 %collective-permute-done.1.refs_6_ = bf16[128,1024]{1,0:T(8,128)(2,1)S(1)} collective-permute-done((bf16[128,1024]{1,0:T(8,128)(2,1)S(1)}, bf16[128,1024]{1,0:T(8,128)(2,1)S(1)}, u32[]{:S(2)}, u32[]{:S(2)}) %collective-permute-start.1) | collective-permute-done | bytes 262176 | tf_op jit(solution)/shard_map/ppermute | solution.py:513
  32.7 1.2 stream_kernel.1
  33.9 2.4 %collective-permute-done.2.refs_1_ = bf16[4,104,1024]{2,1,0:T(8,128)(2,1)S(1)} collective-permute-done((bf16[4,104,1024]{2,1,0:T(8,128)(2,1)S(1)}, bf16[4,104,1024]{2,1,0:T(8,128)(2,1)S(1)}, u32[]{:S(2)}, u32[]{:S(2)}) %collective-permute-start.2) | collective-permute-done | bytes 852000 | tf_op jit(solution)/shard_map/ppermute | solution.py:516
  36.4 1.6 %collective-permute-start.7 = (bf16[2,72,1024]{2,1,0:T(8,128)(2,1)S(1)}, bf16[2,72,1024]{2,1,0:T(8,128)(2,1)S(1)}, u32[]{:S(2)}, u32[]{:S(2)}) collective-permute-start(bf16[2,72,1024]{2,1,0:T(8,128)(2,1)S(1)} %get-tuple-element.94.refs_0_), channel_id=1, source_target_pairs={{0,16},{8,24},{16,0},{24,8},{1,17},{9,25},{17,1},{25,9},{2,18},{10... | collective-permute-start | bytes 884744 | tf_op jit(solution)/shard_map/ppermute | solution.py:513
  38.0 1.5 collective-permute-start.6
  39.5 1.2 collective-permute-start.5
  40.8 2.4 %collective-permute-start.3 = (bf16[2,72,1024]{2,1,0:T(8,128)(2,1)S(1)}, bf16[2,72,1024]{2,1,0:T(8,128)(2,1)S(1)}, u32[]{:S(2)}, u32[]{:S(2)}) collective-permute-start(bf16[2,72,1024]{2,1,0:T(8,128)(2,1)S(1)} %get-tuple-element.92), channel_id=1, source_target_pairs={{0,4},{1,5},{2,6},{3,7},{4,0},{5,1},{6,2},{7,3},{8,12},{9,13},{10,... | collective-permute-start | bytes 884744 | tf_op jit(solution)/shard_map/ppermute | solution.py:516
  43.1 2.4 %collective-permute-done.7.refs_1_.refs_2_ = bf16[2,72,1024]{2,1,0:T(8,128)(2,1)S(1)} collective-permute-done((bf16[2,72,1024]{2,1,0:T(8,128)(2,1)S(1)}, bf16[2,72,1024]{2,1,0:T(8,128)(2,1)S(1)}, u32[]{:S(2)}, u32[]{:S(2)}) %collective-permute-start.7) | collective-permute-done | bytes 294944 | tf_op jit(solution)/shard_map/ppermute | solution.py:513
  45.5 1.2 collective-permute-done.6.refs_0_.refs_1_
  46.8 7.3 %collective-permute-done.5.refs_0_ = bf16[2,72,1024]{2,1,0:T(8,128)(2,1)S(1)} collective-permute-done((bf16[2,72,1024]{2,1,0:T(8,128)(2,1)S(1)}, bf16[2,72,1024]{2,1,0:T(8,128)(2,1)S(1)}, u32[]{:S(2)}, u32[]{:S(2)}) %collective-permute-start.5) | collective-permute-done | bytes 294944 | tf_op jit(solution)/shard_map/ppermute | solution.py:516
  55.2 1.5 collective-permute-start.11
  56.7 1.5 collective-permute-start.10
  58.3 6.7 %collective-permute-done.11.refs_4_.refs_3_ = bf16[1,72,1024]{2,1,0:T(8,128)(2,1)S(1)} collective-permute-done((bf16[1,72,1024]{2,1,0:T(8,128)(2,1)S(1)}, bf16[1,72,1024]{2,1,0:T(8,128)(2,1)S(1)}, u32[]{:S(2)}, u32[]{:S(2)}) %collective-permute-start.11) | collective-permute-done | bytes 147488 | tf_op jit(solution)/shard_map/ppermute | solution.py:513
  65.8 1.5 collective-permute-start.13
  67.3 2.3 %collective-permute-start.4 = (bf16[2,72,1024]{2,1,0:T(8,128)(2,1)S(1)}, bf16[2,72,1024]{2,1,0:T(8,128)(2,1)S(1)}, u32[]{:S(2)}, u32[]{:S(2)}) collective-permute-start(bf16[2,72,1024]{2,1,0:T(8,128)(2,1)S(1)} %hold_farthest.1.refs_5_), channel_id=1, source_target_pairs={{0,6},{1,7},{2,4},{3,5},{4,2},{5,3},{6,0},{7,1},{8,14},{9,15},{10,... | collective-permute-start | bytes 884744 | tf_op jit(solution)/shard_map/ppermute | solution.py:516
  69.6 3.3 %up_0.1 = (f32[288,512]{1,0:T(8,128)S(1)}, f32[288,512]{1,0:T(8,128)S(1)}, f32[288,128]{1,0:T(8,128)S(1)}) custom-call(s32[1]{0:T(128)} %bitcast.refs_0_.me, bf16[2,72,1024]{2,1,0:T(8,128)(2,1)S(1)} %get-tuple-element.94.refs_0_, bf16[2,72,1024]{2,1,0:T(8,128)(2,1)S(1)} %collective-permute-done.6.refs_0_.refs_1_, ...), custom_call_target="tpu_custom_call" | custom-call | tf_op jit(solution)/shard_map/up_0/pallas_call | solution.py:279
  72.9 3.1 %collective-permute-done.4.refs_0_ = bf16[2,72,1024]{2,1,0:T(8,128)(2,1)S(1)} collective-permute-done((bf16[2,72,1024]{2,1,0:T(8,128)(2,1)S(1)}, bf16[2,72,1024]{2,1,0:T(8,128)(2,1)S(1)}, u32[]{:S(2)}, u32[]{:S(2)}) %collective-permute-start.4) | collective-permute-done | bytes 294944 | tf_op jit(solution)/shard_map/ppermute | solution.py:516
  76.0 1.6 %collective-permute-start.14 = (bf16[3,72,1024]{2,1,0:T(8,128)(2,1)S(1)}, bf16[3,72,1024]{2,1,0:T(8,128)(2,1)S(1)}, u32[]{:S(2)}, u32[]{:S(2)}) collective-permute-start(bf16[3,72,1024]{2,1,0:T(8,128)(2,1)S(1)} %get-tuple-element.100), channel_id=1, source_target_pairs={{0,8},{8,0},{16,24},{24,16},{1,9},{9,1},{17,25},{25,17},{2,10},{10... | collective-permute-start | bytes 1327112 | tf_op jit(solution)/shard_map/ppermute | solution.py:510
  77.6 1.3 collective-permute-start.15
  78.9 3.2 %up_1.1 = (f32[288,512]{1,0:T(8,128)S(1)}, f32[288,512]{1,0:T(8,128)S(1)}, f32[288,128]{1,0:T(8,128)S(1)}) custom-call(s32[1]{0:T(128)} %bitcast.refs_0_.me, bf16[2,72,1024]{2,1,0:T(8,128)(2,1)S(1)} %hold_near.1.refs_0_, bf16[2,72,1024]{2,1,0:T(8,128)(2,1)S(1)} %collective-permute-done.8.refs_1_, ...), custom_call_target="tpu_custom_call", output_to_operand_aliasing={{0}: (9, {}), {1}: (10, {}), {2}: (11, {})} | custom-call | tf_op jit(solution)/shard_map/up_1/pallas_call | solution.py:279
  82.1 2.6 %collective-permute-done.14.refs_0_.refs_4_.refs_1_ = bf16[3,72,1024]{2,1,0:T(8,128)(2,1)S(1)} collective-permute-done((bf16[3,72,1024]{2,1,0:T(8,128)(2,1)S(1)}, bf16[3,72,1024]{2,1,0:T(8,128)(2,1)S(1)}, u32[]{:S(2)}, u32[]{:S(2)}) %collective-permute-start.14) | collective-permute-done | bytes 442400 | tf_op jit(solution)/shard_map/ppermute | solution.py:510
  84.7 2.8 %collective-permute-done.15.refs_1_.refs_3_.refs_2_ = bf16[3,72,1024]{2,1,0:T(8,128)(2,1)S(1)} collective-permute-done((bf16[3,72,1024]{2,1,0:T(8,128)(2,1)S(1)}, bf16[3,72,1024]{2,1,0:T(8,128)(2,1)S(1)}, u32[]{:S(2)}, u32[]{:S(2)}) %collective-permute-start.15) | collective-permute-done | bytes 442400 | tf_op jit(solution)/shard_map/ppermute | solution.py:513
  87.5 1.3 collective-permute-start.16
  89.3 3.2 %up_2.1 = (f32[288,512]{1,0:T(8,128)S(1)}, f32[288,512]{1,0:T(8,128)S(1)}, f32[288,128]{1,0:T(8,128)S(1)}) custom-call(s32[1]{0:T(128)} %bitcast.refs_0_.me, bf16[2,72,1024]{2,1,0:T(8,128)(2,1)S(1)} %collective-permute-done.3.refs_1_.refs_0_, ...), custom_call_target="tpu_custom_call", output_to_operand_aliasing={{0}: (9, {}), {1}: (10, {}), {2}: (11, {})} | custom-call | tf_op jit(solution)/shard_map/up_2/pallas_call | solution.py:279
  92.7 1.3 collective-permute-done.17.refs_4_
  94.0 3.5 %up_3.1 = (bf16[72,512]{1,0:T(8,128)(2,1)S(1)}, bf16[216,512]{1,0:T(8,128)(2,1)S(1)}) custom-call(s32[1]{0:T(128)} %bitcast.refs_0_.me, bf16[2,72,1024]{2,1,0:T(8,128)(2,1)S(1)} %collective-permute-done.4.refs_0_, bf16[3,72,1024]{2,1,0:T(8,128)(2,1)S(1)} %collective-permute-done.14.refs_0_.refs_4_.refs_1_, ...), custom_call_target="tpu_custom_call" | custom-call | tf_op jit(solution)/shard_map/up_3/pallas_call | solution.py:279
  97.6 6.9 %down_through.1 = (bf16[9,16,1024]{2,1,0:T(8,128)(2,1)S(1)}, bf16[9,16,1024]{2,1,0:T(8,128)(2,1)S(1)}, bf16[9,16,1024]{2,1,0:T(8,128)(2,1)S(1)}, bf16[9,16,1024]{2,1,0:T(8,128)(2,1)S(1)}) custom-call(bf16[72,512]{1,0:T(8,128)(2,1)S(1)} %get-tuple-element.120.act_ref, bf16[512,8192]{1,0:T(8,128)(2,1)} %bitcast.27), custom_call_target="tpu_custom_call" | custom-call | tf_op jit(solution)/shard_map/down_through/pallas_call | solution.py:357
  104.9 0.9 collective-permute-start.19
  105.8 3.9 %collective-permute-start.21 = (bf16[2,32,1024]{2,1,0:T(8,128)(2,1)S(1)}, bf16[2,32,1024]{2,1,0:T(8,128)(2,1)S(1)}, u32[]{:S(2)}, u32[]{:S(2)}) collective-permute-start(bf16[2,32,1024]{2,1,0:T(8,128)(2,1)S(1)} %get-tuple-element.129), channel_id=1, source_target_pairs={{0,4},{1,5},{2,6},{3,7},{4,0},{5,1},{6,2},{7,3},{8,12},{9,13},{10,... | collective-permute-start | bytes 393224 | tf_op jit(solution)/shard_map/ppermute | solution.py:516
  109.7 1.4 collective-permute-start.22
  111.2 7.6 %down_rest.1 = (bf16[9,16,1024]{2,1,0:T(8,128)(2,1)S(1)}, bf16[9,16,1024]{2,1,0:T(8,128)(2,1)S(1)}, bf16[9,16,1024]{2,1,0:T(8,128)(2,1)S(1)}, bf16[9,16,1024]{2,...) custom-call(bf16[216,512]{1,0:T(8,128)(2,1)S(1)} %get-tuple-element., ...), custom_call_target="tpu_custom_call" | custom-call | tf_op jit(solution)/shard_map/down_rest/pallas_call | solution.py:357
  119.0 1.6 %collective-permute-start.23 = (bf16[9,16,1024]{2,1,0:T(8,128)(2,1)S(1)}, bf16[9,16,1024]{2,1,0:T(8,128)(2,1)S(1)}, u32[]{:S(2)}, u32[]{:S(2)}) collective-permute-start(bf16[9,16,1024]{2,1,0:T(8,128)(2,1)S(1)} %get-tuple-element.131), channel_id=1, source_target_pairs={{0,8},{8,0},{16,24},{24,16},{1,9},{9,1},{17,25},{25,17},{2,10},{10... | collective-permute-start | bytes 884744 | tf_op jit(solution)/shard_map/ppermute | solution.py:510
  121.7 1.4 collective-permute-start.28
  123.2 5.9 %collective-permute-done.23.refs_1_ = bf16[9,16,1024]{2,1,0:T(8,128)(2,1)S(1)} collective-permute-done((bf16[9,16,1024]{2,1,0:T(8,128)(2,1)S(1)}, bf16[9,16,1024]{2,1,0:T(8,128)(2,1)S(1)}, u32[]{:S(2)}, u32[]{:S(2)}) %collective-permute-start.23) | collective-permute-done | bytes 294944 | tf_op jit(solution)/shard_map/ppermute | solution.py:510
  129.0 1.4 collective-permute-done.24.refs_2_
  130.6 0.7 collective-permute-start.25
  131.5 2.8 %collective-permute-start.33 = (bf16[9,16,1024]{2,1,0:T(8,128)(2,1)S(1)}, bf16[9,16,1024]{2,1,0:T(8,128)(2,1)S(1)}, u32[]{:S(2)}, u32[]{:S(2)}) collective-permute-start(bf16[9,16,1024]{2,1,0:T(8,128)(2,1)S(1)} %get-tuple-element.143.refs_6_), channel_id=1, source_target_pairs={{0,6},{1,7},{2,4},{3,5},{4,2},{5,3},{6,0},{7,1},{8,14},{9,15},{10,... | collective-permute-start | bytes 884744 | tf_op jit(solution)/shard_map/ppermute | solution.py:516
  134.3 0.9 collective-permute-done.27.refs_0_
  135.2 0.9 collective-permute-done.28.refs_1_
  136.2 0.9 collective-permute-start.31
  138.4 0.9 collective-permute-done.26.refs_2_
  139.4 0.9 collective-permute-start.29
  140.3 1.0 collective-permute-start.30
  141.3 3.4 %collective-permute-start.35 = (bf16[9,16,1024]{2,1,0:T(8,128)(2,1)S(1)}, bf16[9,16,1024]{2,1,0:T(8,128)(2,1)S(1)}, u32[]{:S(2)}, u32[]{:S(2)}) collective-permute-start(bf16[9,16,1024]{2,1,0:T(8,128)(2,1)S(1)} %get-tuple-element.151), channel_id=1, source_target_pairs={{0,4},{1,5},{2,6},{3,7},{4,0},{5,1},{6,2},{7,3},{8,12},{9,13},{10,... | collective-permute-start | bytes 884744 | tf_op jit(solution)/shard_map/ppermute | solution.py:516
  144.8 0.7 collective-permute-start.34
  146.2 0.9 collective-permute-done.30.refs_2_
  147.2 5.5 %collective-permute-done.35.refs_2_.refs_6_ = bf16[9,16,1024]{2,1,0:T(8,128)(2,1)S(1)} collective-permute-done((bf16[9,16,1024]{2,1,0:T(8,128)(2,1)S(1)}, bf16[9,16,1024]{2,1,0:T(8,128)(2,1)S(1)}, u32[]{:S(2)}, u32[]{:S(2)}) %collective-permute-start.35) | collective-permute-done | bytes 294944 | tf_op jit(solution)/shard_map/ppermute | solution.py:516
  153.4 2.0 %collective-permute-done.36.refs_3_ = bf16[2,9,16,1024]{3,2,1,0:T(8,128)(2,1)S(1)} collective-permute-done((bf16[2,9,16,1024]{3,2,1,0:T(8,128)(2,1)S(1)}, bf16[2,9,16,1024]{3,2,1,0:T(8,128)(2,1)S(1)}, u32[]{:S(2)}, u32[]{:S(2)}) %collective-permute-start.36) | collective-permute-done | bytes 589856 | tf_op jit(solution)/shard_map/ppermute | solution.py:516
  155.4 1.9 %mix_kernel.1 = bf16[32,8192]{1,0:T(8,128)(2,1)} custom-call(s32[1]{0:T(128)} %bitcast.refs_0_.me, s32[2,32]{1,0:T(2,128)S(1)} %bitcast.17, f32[2,32]{1,0:T(2,128)S(1)} %bitcast.18, bf16[2,9,16,1024]{3,2,1,0:T(8,128)(2,1)S(1)} %collective-permute-done.36.refs_3_, bf16[9,16,1024]{2,1,0:T(8,128)(2,1)S(1)} %finish_0.1.refs_0_.refs_4_, ...), custom_call_target="tpu_custom_call" | custom-call | tf_op jit(solution)/shard_map/mix_kernel/pallas_call | solution.py:39
  (62 shorter events, 8.5 us)
Async XLA Ops:
  0.0 1.0 copy-start.3
  1.0 0.7 copy-start.8
  2.8 66.9 %copy-start.2 = (f32[8192]{0:T(1024)S(1)}, f32[8192]{0:T(1024)}, u32[]{:S(2)}) copy-start(f32[8192]{0:T(1024)} %param.24) | copy-start | bytes 98308
  2.8 23.5 %all-to-all-start = ((bf16[8,32,1152]{2,1,0:T(8,128)(2,1)}), bf16[8,32,1152]{2,1,0:T(8,128)(2,1)S(1)}, u32[]{:S(2)}, u32[]{:S(2)}) async-start(bf16[8,32,1152]{2,1,0:T(8,128)(2,1)} %pack_kernel.1), calls=%async_computation | async-start | bytes 1179648 | tf_op jit(solution)/shard_map/all_to_all | solution.py:529
  13.2 9.7 %collective-permute-start = (bf16[144,1024]{1,0:T(8,128)(2,1)}, bf16[144,1024]{1,0:T(8,128)(2,1)S(1)}, u32[]{:S(2)}, u32[]{:S(2)}) collective-permute-start(bf16[144,1024]{1,0:T(8,128)(2,1)} %get-tuple-element.82.refs_1_), channel_id=1, source_target_pairs={{0,8},{8,0},{16,24},{24,16},{1,9},{9,1},{17,25},{25,17},{2,10},{10... | collective-permute-start | bytes 884744 | tf_op jit(solution)/shard_map/ppermute | solution.py:510
  22.9 1.0 copy-start.4
  23.9 0.7 copy-start.7
  24.7 8.0 %collective-permute-start.1 = (bf16[128,1024]{1,0:T(8,128)(2,1)S(1)}, bf16[128,1024]{1,0:T(8,128)(2,1)S(1)}, u32[]{:S(2)}, u32[]{:S(2)}) collective-permute-start(bf16[128,1024]{1,0:T(8,128)(2,1)S(1)} %join_kernel.1.refs_6_), channel_id=1, source_target_pairs={{0,16},{8,24},{16,0},{24,8},{1,17},{9,25},{17,1},{25,9},{2,18},{10... | collective-permute-start | bytes 786440 | tf_op jit(solution)/shard_map/ppermute | solution.py:513
  26.3 1.2 copy-start
  27.5 1.2 copy-start.1
  28.7 0.9 copy-start.5
  29.7 0.8 copy-start.6
  33.9 2.4 %collective-permute-start.2 = (bf16[4,104,1024]{2,1,0:T(8,128)(2,1)S(1)}, bf16[4,104,1024]{2,1,0:T(8,128)(2,1)S(1)}, u32[]{:S(2)}, u32[]{:S(2)}) collective-permute-start(bf16[4,104,1024]{2,1,0:T(8,128)(2,1)S(1)} %get-tuple-element.90), channel_id=1, source_target_pairs={{0,1},{1,0},{2,3},{3,2},{4,5},{5,4},{6,7},{7,6},{8,9},{9,8},{10,11... | collective-permute-start | bytes 2555912 | tf_op jit(solution)/shard_map/ppermute | solution.py:516
  36.4 9.1 %collective-permute-start.7 = (bf16[2,72,1024]{2,1,0:T(8,128)(2,1)S(1)}, bf16[2,72,1024]{2,1,0:T(8,128)(2,1)S(1)}, u32[]{:S(2)}, u32[]{:S(2)}) collective-permute-start(bf16[2,72,1024]{2,1,0:T(8,128)(2,1)S(1)} %get-tuple-element.94.refs_0_), channel_id=1, source_target_pairs={{0,16},{8,24},{16,0},{24,8},{1,17},{9,25},{17,1},{25,9},{2,18},{10... | collective-permute-start | bytes 884744 | tf_op jit(solution)/shard_map/ppermute | solution.py:513
  38.0 8.8 %collective-permute-start.6 = (bf16[2,72,1024]{2,1,0:T(8,128)(2,1)S(1)}, bf16[2,72,1024]{2,1,0:T(8,128)(2,1)S(1)}, u32[]{:S(2)}, u32[]{:S(2)}) collective-permute-start(bf16[2,72,1024]{2,1,0:T(8,128)(2,1)S(1)} %get-tuple-element.94.refs_0_), channel_id=1, source_target_pairs={{0,8},{8,0},{16,24},{24,16},{1,9},{9,1},{17,25},{25,17},{2,10},{10... | collective-permute-start | bytes 884744 | tf_op jit(solution)/shard_map/ppermute | solution.py:510
  39.5 14.6 %collective-permute-start.5 = (bf16[2,72,1024]{2,1,0:T(8,128)(2,1)S(1)}, bf16[2,72,1024]{2,1,0:T(8,128)(2,1)S(1)}, u32[]{:S(2)}, u32[]{:S(2)}) collective-permute-start(bf16[2,72,1024]{2,1,0:T(8,128)(2,1)S(1)} %get-tuple-element.93), channel_id=1, source_target_pairs={{0,2},{1,3},{2,0},{3,1},{4,6},{5,7},{6,4},{7,5},{8,10},{9,11},{10,... | collective-permute-start | bytes 884744 | tf_op jit(solution)/shard_map/ppermute | solution.py:516
  40.8 17.5 %collective-permute-start.3 = (bf16[2,72,1024]{2,1,0:T(8,128)(2,1)S(1)}, bf16[2,72,1024]{2,1,0:T(8,128)(2,1)S(1)}, u32[]{:S(2)}, u32[]{:S(2)}) collective-permute-start(bf16[2,72,1024]{2,1,0:T(8,128)(2,1)S(1)} %get-tuple-element.92), channel_id=1, source_target_pairs={{0,4},{1,5},{2,6},{3,7},{4,0},{5,1},{6,2},{7,3},{8,12},{9,13},{10,... | collective-permute-start | bytes 884744 | tf_op jit(solution)/shard_map/ppermute | solution.py:516
  54.1 11.0 %collective-permute-start.9 = (bf16[2,72,1024]{2,1,0:T(8,128)(2,1)S(1)}, bf16[2,72,1024]{2,1,0:T(8,128)(2,1)S(1)}, u32[]{:S(2)}, u32[]{:S(2)}) collective-permute-start(bf16[2,72,1024]{2,1,0:T(8,128)(2,1)S(1)} %hold_near.1.refs_0_), channel_id=1, source_target_pairs={{0,16},{8,24},{16,0},{24,8},{1,17},{9,25},{17,1},{25,9},{2,18},{10... | collective-permute-start | bytes 884744 | tf_op jit(solution)/shard_map/ppermute | solution.py:513
  54.7 10.5 %collective-permute-start.8 = (bf16[2,72,1024]{2,1,0:T(8,128)(2,1)S(1)}, bf16[2,72,1024]{2,1,0:T(8,128)(2,1)S(1)}, u32[]{:S(2)}, u32[]{:S(2)}) collective-permute-start(bf16[2,72,1024]{2,1,0:T(8,128)(2,1)S(1)} %hold_near.1.refs_0_), channel_id=1, source_target_pairs={{0,8},{8,0},{16,24},{24,16},{1,9},{9,1},{17,25},{25,17},{2,10},{10... | collective-permute-start | bytes 884744 | tf_op jit(solution)/shard_map/ppermute | solution.py:510
  55.2 9.7 %collective-permute-start.11 = (bf16[1,72,1024]{2,1,0:T(8,128)(2,1)S(1)}, bf16[1,72,1024]{2,1,0:T(8,128)(2,1)S(1)}, u32[]{:S(2)}, u32[]{:S(2)}) collective-permute-start(bf16[1,72,1024]{2,1,0:T(8,128)(2,1)S(1)} %get-tuple-element.96), channel_id=1, source_target_pairs={{0,16},{8,24},{16,0},{24,8},{1,17},{9,25},{17,1},{25,9},{2,18},{10... | collective-permute-start | bytes 442376 | tf_op jit(solution)/shard_map/ppermute | solution.py:513
  56.7 8.4 %collective-permute-start.10 = (bf16[1,72,1024]{2,1,0:T(8,128)(2,1)S(1)}, bf16[1,72,1024]{2,1,0:T(8,128)(2,1)S(1)}, u32[]{:S(2)}, u32[]{:S(2)}) collective-permute-start(bf16[1,72,1024]{2,1,0:T(8,128)(2,1)S(1)} %get-tuple-element.95.refs_1_), channel_id=1, source_target_pairs={{0,8},{8,0},{16,24},{24,16},{1,9},{9,1},{17,25},{25,17},{2,10},{10... | collective-permute-start | bytes 442376 | tf_op jit(solution)/shard_map/ppermute | solution.py:510
  65.2 10.7 %collective-permute-start.12 = (bf16[3,72,1024]{2,1,0:T(8,128)(2,1)S(1)}, bf16[3,72,1024]{2,1,0:T(8,128)(2,1)S(1)}, u32[]{:S(2)}, u32[]{:S(2)}) collective-permute-start(bf16[3,72,1024]{2,1,0:T(8,128)(2,1)S(1)} %get-tuple-element.97), channel_id=1, source_target_pairs={{0,8},{8,0},{16,24},{24,16},{1,9},{9,1},{17,25},{25,17},{2,10},{10... | collective-permute-start | bytes 1327112 | tf_op jit(solution)/shard_map/ppermute | solution.py:510
  65.8 10.2 %collective-permute-start.13 = (bf16[3,72,1024]{2,1,0:T(8,128)(2,1)S(1)}, bf16[3,72,1024]{2,1,0:T(8,128)(2,1)S(1)}, u32[]{:S(2)}, u32[]{:S(2)}) collective-permute-start(bf16[3,72,1024]{2,1,0:T(8,128)(2,1)S(1)} %get-tuple-element.98), channel_id=1, source_target_pairs={{0,16},{8,24},{16,0},{24,8},{1,17},{9,25},{17,1},{25,9},{2,18},{10... | collective-permute-start | bytes 1327112 | tf_op jit(solution)/shard_map/ppermute | solution.py:513
  67.3 8.6 %collective-permute-start.4 = (bf16[2,72,1024]{2,1,0:T(8,128)(2,1)S(1)}, bf16[2,72,1024]{2,1,0:T(8,128)(2,1)S(1)}, u32[]{:S(2)}, u32[]{:S(2)}) collective-permute-start(bf16[2,72,1024]{2,1,0:T(8,128)(2,1)S(1)} %hold_farthest.1.refs_5_), channel_id=1, source_target_pairs={{0,6},{1,7},{2,4},{3,5},{4,2},{5,3},{6,0},{7,1},{8,14},{9,15},{10,... | collective-permute-start | bytes 884744 | tf_op jit(solution)/shard_map/ppermute | solution.py:516
  76.0 8.6 %collective-permute-start.14 = (bf16[3,72,1024]{2,1,0:T(8,128)(2,1)S(1)}, bf16[3,72,1024]{2,1,0:T(8,128)(2,1)S(1)}, u32[]{:S(2)}, u32[]{:S(2)}) collective-permute-start(bf16[3,72,1024]{2,1,0:T(8,128)(2,1)S(1)} %get-tuple-element.100), channel_id=1, source_target_pairs={{0,8},{8,0},{16,24},{24,16},{1,9},{9,1},{17,25},{25,17},{2,10},{10... | collective-permute-start | bytes 1327112 | tf_op jit(solution)/shard_map/ppermute | solution.py:510
  77.6 9.9 %collective-permute-start.15 = (bf16[3,72,1024]{2,1,0:T(8,128)(2,1)S(1)}, bf16[3,72,1024]{2,1,0:T(8,128)(2,1)S(1)}, u32[]{:S(2)}, u32[]{:S(2)}) collective-permute-start(bf16[3,72,1024]{2,1,0:T(8,128)(2,1)S(1)} %get-tuple-element.101), channel_id=1, source_target_pairs={{0,16},{8,24},{16,0},{24,8},{1,17},{9,25},{17,1},{25,9},{2,18},{10... | collective-permute-start | bytes 1327112 | tf_op jit(solution)/shard_map/ppermute | solution.py:513
  87.5 5.2 %collective-permute-start.16 = (bf16[1,72,1024]{2,1,0:T(8,128)(2,1)S(1)}, bf16[1,72,1024]{2,1,0:T(8,128)(2,1)S(1)}, u32[]{:S(2)}, u32[]{:S(2)}) collective-permute-start(bf16[1,72,1024]{2,1,0:T(8,128)(2,1)S(1)} %get-tuple-element.105), channel_id=1, source_target_pairs={{0,16},{8,24},{16,0},{24,8},{1,17},{9,25},{17,1},{25,9},{2,18},{10... | collective-permute-start | bytes 442376 | tf_op jit(solution)/shard_map/ppermute | solution.py:513
  88.9 5.1 %collective-permute-start.17 = (bf16[1,72,1024]{2,1,0:T(8,128)(2,1)S(1)}, bf16[1,72,1024]{2,1,0:T(8,128)(2,1)S(1)}, u32[]{:S(2)}, u32[]{:S(2)}) collective-permute-start(bf16[1,72,1024]{2,1,0:T(8,128)(2,1)S(1)} %get-tuple-element.106.refs_3_), channel_id=1, source_target_pairs={{0,8},{8,0},{16,24},{24,16},{1,9},{9,1},{17,25},{25,17},{2,10},{10... | collective-permute-start | bytes 442376 | tf_op jit(solution)/shard_map/ppermute | solution.py:510
  104.5 14.4 %collective-permute-start.18 = (bf16[9,16,1024]{2,1,0:T(8,128)(2,1)S(1)}, bf16[9,16,1024]{2,1,0:T(8,128)(2,1)S(1)}, u32[]{:S(2)}, u32[]{:S(2)}) collective-permute-start(bf16[9,16,1024]{2,1,0:T(8,128)(2,1)S(1)} %get-tuple-element.121), channel_id=1, source_target_pairs={{0,8},{8,0},{16,24},{24,16},{1,9},{9,1},{17,25},{25,17},{2,10},{10... | collective-permute-start | bytes 884744 | tf_op jit(solution)/shard_map/ppermute | solution.py:510
  104.9 13.9 %collective-permute-start.19 = (bf16[9,16,1024]{2,1,0:T(8,128)(2,1)S(1)}, bf16[9,16,1024]{2,1,0:T(8,128)(2,1)S(1)}, u32[]{:S(2)}, u32[]{:S(2)}) collective-permute-start(bf16[9,16,1024]{2,1,0:T(8,128)(2,1)S(1)} %get-tuple-element.122), channel_id=1, source_target_pairs={{0,16},{8,24},{16,0},{24,8},{1,17},{9,25},{17,1},{25,9},{2,18},{10... | collective-permute-start | bytes 884744 | tf_op jit(solution)/shard_map/ppermute | solution.py:513
  105.8 13.0 %collective-permute-start.21 = (bf16[2,32,1024]{2,1,0:T(8,128)(2,1)S(1)}, bf16[2,32,1024]{2,1,0:T(8,128)(2,1)S(1)}, u32[]{:S(2)}, u32[]{:S(2)}) collective-permute-start(bf16[2,32,1024]{2,1,0:T(8,128)(2,1)S(1)} %get-tuple-element.129), channel_id=1, source_target_pairs={{0,4},{1,5},{2,6},{3,7},{4,0},{5,1},{6,2},{7,3},{8,12},{9,13},{10,... | collective-permute-start | bytes 393224 | tf_op jit(solution)/shard_map/ppermute | solution.py:516
  109.7 9.1 %collective-permute-start.22 = (bf16[2,32,1024]{2,1,0:T(8,128)(2,1)S(1)}, bf16[2,32,1024]{2,1,0:T(8,128)(2,1)S(1)}, u32[]{:S(2)}, u32[]{:S(2)}) collective-permute-start(bf16[2,32,1024]{2,1,0:T(8,128)(2,1)S(1)} %get-tuple-element.130), channel_id=1, source_target_pairs={{0,6},{1,7},{2,4},{3,5},{4,2},{5,3},{6,0},{7,1},{8,14},{9,15},{10,... | collective-permute-start | bytes 393224 | tf_op jit(solution)/shard_map/ppermute | solution.py:516
  111.2 7.7 %collective-permute-start.20 = (bf16[2,32,1024]{2,1,0:T(8,128)(2,1)S(1)}, bf16[2,32,1024]{2,1,0:T(8,128)(2,1)S(1)}, u32[]{:S(2)}, u32[]{:S(2)}) collective-permute-start(bf16[2,32,1024]{2,1,0:T(8,128)(2,1)S(1)} %get-tuple-element.112.refs_11_), channel_id=1, source_target_pairs={{0,2},{1,3},{2,0},{3,1},{4,6},{5,7},{6,4},{7,5},{8,10},{9,11},{10,... | collective-permute-start | bytes 393224 | tf_op jit(solution)/shard_map/ppermute | solution.py:516
  111.2 44.2 %copy-start.9 = (s32[32,2]{0,1:T(2,128)S(1)}, s32[32,2]{0,1:T(2,128)}, u32[]{:S(2)}) copy-start(s32[32,2]{0,1:T(2,128)} %param.25) | copy-start | bytes 772
  111.2 44.2 %copy-start.10 = (f32[32,2]{0,1:T(2,128)S(1)}, f32[32,2]{0,1:T(2,128)}, u32[]{:S(2)}) copy-start(f32[32,2]{0,1:T(2,128)} %param.26) | copy-start | bytes 772
  119.0 10.0 %collective-permute-start.23 = (bf16[9,16,1024]{2,1,0:T(8,128)(2,1)S(1)}, bf16[9,16,1024]{2,1,0:T(8,128)(2,1)S(1)}, u32[]{:S(2)}, u32[]{:S(2)}) collective-permute-start(bf16[9,16,1024]{2,1,0:T(8,128)(2,1)S(1)} %get-tuple-element.131), channel_id=1, source_target_pairs={{0,8},{8,0},{16,24},{24,16},{1,9},{9,1},{17,25},{25,17},{2,10},{10... | collective-permute-start | bytes 884744 | tf_op jit(solution)/shard_map/ppermute | solution.py:510
  120.6 9.8 %collective-permute-start.24 = (bf16[9,16,1024]{2,1,0:T(8,128)(2,1)S(1)}, bf16[9,16,1024]{2,1,0:T(8,128)(2,1)S(1)}, u32[]{:S(2)}, u32[]{:S(2)}) collective-permute-start(bf16[9,16,1024]{2,1,0:T(8,128)(2,1)S(1)} %get-tuple-element.132), channel_id=1, source_target_pairs={{0,16},{8,24},{16,0},{24,8},{1,17},{9,25},{17,1},{25,9},{2,18},{10... | collective-permute-start | bytes 884744 | tf_op jit(solution)/shard_map/ppermute | solution.py:513
  121.2 14.0 %collective-permute-start.27 = (bf16[9,16,1024]{2,1,0:T(8,128)(2,1)S(1)}, bf16[9,16,1024]{2,1,0:T(8,128)(2,1)S(1)}, u32[]{:S(2)}, u32[]{:S(2)}) collective-permute-start(bf16[9,16,1024]{2,1,0:T(8,128)(2,1)S(1)} %get-tuple-element.137), channel_id=1, source_target_pairs={{0,8},{8,0},{16,24},{24,16},{1,9},{9,1},{17,25},{25,17},{2,10},{10... | collective-permute-start | bytes 884744 | tf_op jit(solution)/shard_map/ppermute | solution.py:510
  121.7 14.4 %collective-permute-start.28 = (bf16[9,16,1024]{2,1,0:T(8,128)(2,1)S(1)}, bf16[9,16,1024]{2,1,0:T(8,128)(2,1)S(1)}, u32[]{:S(2)}, u32[]{:S(2)}) collective-permute-start(bf16[9,16,1024]{2,1,0:T(8,128)(2,1)S(1)} %get-tuple-element.138), channel_id=1, source_target_pairs={{0,16},{8,24},{16,0},{24,8},{1,17},{9,25},{17,1},{25,9},{2,18},{10... | collective-permute-start | bytes 884744 | tf_op jit(solution)/shard_map/ppermute | solution.py:513
  130.6 7.8 %collective-permute-start.25 = (bf16[9,16,1024]{2,1,0:T(8,128)(2,1)S(1)}, bf16[9,16,1024]{2,1,0:T(8,128)(2,1)S(1)}, u32[]{:S(2)}, u32[]{:S(2)}) collective-permute-start(bf16[9,16,1024]{2,1,0:T(8,128)(2,1)S(1)} %get-tuple-element.135), channel_id=1, source_target_pairs={{0,8},{8,0},{16,24},{24,16},{1,9},{9,1},{17,25},{25,17},{2,10},{10... | collective-permute-start | bytes 884744 | tf_op jit(solution)/shard_map/ppermute | solution.py:510
  131.3 8.0 %collective-permute-start.26 = (bf16[9,16,1024]{2,1,0:T(8,128)(2,1)S(1)}, bf16[9,16,1024]{2,1,0:T(8,128)(2,1)S(1)}, u32[]{:S(2)}, u32[]{:S(2)}) collective-permute-start(bf16[9,16,1024]{2,1,0:T(8,128)(2,1)S(1)} %get-tuple-element.136), channel_id=1, source_target_pairs={{0,16},{8,24},{16,0},{24,8},{1,17},{9,25},{17,1},{25,9},{2,18},{10... | collective-permute-start | bytes 884744 | tf_op jit(solution)/shard_map/ppermute | solution.py:513
  131.5 9.8 %collective-permute-start.33 = (bf16[9,16,1024]{2,1,0:T(8,128)(2,1)S(1)}, bf16[9,16,1024]{2,1,0:T(8,128)(2,1)S(1)}, u32[]{:S(2)}, u32[]{:S(2)}) collective-permute-start(bf16[9,16,1024]{2,1,0:T(8,128)(2,1)S(1)} %get-tuple-element.143.refs_6_), channel_id=1, source_target_pairs={{0,6},{1,7},{2,4},{3,5},{4,2},{5,3},{6,0},{7,1},{8,14},{9,15},{10,... | collective-permute-start | bytes 884744 | tf_op jit(solution)/shard_map/ppermute | solution.py:516
  136.2 8.5 %collective-permute-start.31 = (bf16[9,16,1024]{2,1,0:T(8,128)(2,1)S(1)}, bf16[9,16,1024]{2,1,0:T(8,128)(2,1)S(1)}, u32[]{:S(2)}, u32[]{:S(2)}) collective-permute-start(bf16[9,16,1024]{2,1,0:T(8,128)(2,1)S(1)} %get-tuple-element.149), channel_id=1, source_target_pairs={{0,8},{8,0},{16,24},{24,16},{1,9},{9,1},{17,25},{25,17},{2,10},{10... | collective-permute-start | bytes 884744 | tf_op jit(solution)/shard_map/ppermute | solution.py:510
  137.2 7.5 %collective-permute-start.32 = (bf16[9,16,1024]{2,1,0:T(8,128)(2,1)S(1)}, bf16[9,16,1024]{2,1,0:T(8,128)(2,1)S(1)}, u32[]{:S(2)}, u32[]{:S(2)}) collective-permute-start(bf16[9,16,1024]{2,1,0:T(8,128)(2,1)S(1)} %get-tuple-element.150), channel_id=1, source_target_pairs={{0,16},{8,24},{16,0},{24,8},{1,17},{9,25},{17,1},{25,9},{2,18},{10... | collective-permute-start | bytes 884744 | tf_op jit(solution)/shard_map/ppermute | solution.py:513
  139.4 6.8 %collective-permute-start.29 = (bf16[9,16,1024]{2,1,0:T(8,128)(2,1)S(1)}, bf16[9,16,1024]{2,1,0:T(8,128)(2,1)S(1)}, u32[]{:S(2)}, u32[]{:S(2)}) collective-permute-start(bf16[9,16,1024]{2,1,0:T(8,128)(2,1)S(1)} %get-tuple-element.146), channel_id=1, source_target_pairs={{0,8},{8,0},{16,24},{24,16},{1,9},{9,1},{17,25},{25,17},{2,10},{10... | collective-permute-start | bytes 884744 | tf_op jit(solution)/shard_map/ppermute | solution.py:510
  140.3 6.7 %collective-permute-start.30 = (bf16[9,16,1024]{2,1,0:T(8,128)(2,1)S(1)}, bf16[9,16,1024]{2,1,0:T(8,128)(2,1)S(1)}, u32[]{:S(2)}, u32[]{:S(2)}) collective-permute-start(bf16[9,16,1024]{2,1,0:T(8,128)(2,1)S(1)} %get-tuple-element.147), channel_id=1, source_target_pairs={{0,16},{8,24},{16,0},{24,8},{1,17},{9,25},{17,1},{25,9},{2,18},{10... | collective-permute-start | bytes 884744 | tf_op jit(solution)/shard_map/ppermute | solution.py:513
  141.3 11.4 %collective-permute-start.35 = (bf16[9,16,1024]{2,1,0:T(8,128)(2,1)S(1)}, bf16[9,16,1024]{2,1,0:T(8,128)(2,1)S(1)}, u32[]{:S(2)}, u32[]{:S(2)}) collective-permute-start(bf16[9,16,1024]{2,1,0:T(8,128)(2,1)S(1)} %get-tuple-element.151), channel_id=1, source_target_pairs={{0,4},{1,5},{2,6},{3,7},{4,0},{5,1},{6,2},{7,3},{8,12},{9,13},{10,... | collective-permute-start | bytes 884744 | tf_op jit(solution)/shard_map/ppermute | solution.py:516
  144.8 8.4 %collective-permute-start.34 = (bf16[9,16,1024]{2,1,0:T(8,128)(2,1)S(1)}, bf16[9,16,1024]{2,1,0:T(8,128)(2,1)S(1)}, u32[]{:S(2)}, u32[]{:S(2)}) collective-permute-start(bf16[9,16,1024]{2,1,0:T(8,128)(2,1)S(1)} %finish_1.1), channel_id=1, source_target_pairs={{0,2},{1,3},{2,0},{3,1},{4,6},{5,7},{6,4},{7,5},{8,10},{9,11},{10,... | collective-permute-start | bytes 884744 | tf_op jit(solution)/shard_map/ppermute | solution.py:516
  153.3 2.1 %collective-permute-start.36 = (bf16[2,9,16,1024]{3,2,1,0:T(8,128)(2,1)S(1)}, bf16[2,9,16,1024]{3,2,1,0:T(8,128)(2,1)S(1)}, u32[]{:S(2)}, u32[]{:S(2)}) collective-permute-start(bf16[2,9,16,1024]{3,2,1,0:T(8,128)(2,1)S(1)} %second_kernel.1), channel_id=1, source_target_pairs={{0,1},{1,0},{2,3},{3,2},{4,5},{5,4},{6,7},{7,6},{8,9},{9,8},{10,11... | collective-permute-start | bytes 1769480 | tf_op jit(solution)/shard_map/ppermute | solution.py:516
where the time goes:
time: 158 us; the launch traced here: 157 us
  waiting for transfers between devices  55.6 us (35%)
  starting transfers between devices  51.5 us (33%)
  Pallas kernels  42.3 us (27%)
  local copies, waits for them, and re-layouts  7.61 us (5%)
    ppermute x11, waiting for transfers between devices, along(): return lax.ppermute(v, 'exp', [(i, i ^ mask) for i in range(owners)])  20.8 us
    ppermute x11, starting transfers between devices, along(): return lax.ppermute(v, 'exp', [(i, i ^ mask) for i in range(owners)])  18.3 us
    ppermute x13, waiting for transfers between devices, over_y(): return lax.ppermute(v, 'seq', [(i, i ^ 2) for i in range(4)])  18 us
    ppermute x13, waiting for transfers between devices, over_x(): return lax.ppermute(v, 'seq', [(i, i ^ 1) for i in range(4)])  16.8 us
    pallas_call x22, Pallas kernels, block_call(): pl.pallas_call(kernel, name=name or getattr(body, 'func', body).__name__,...  14.6 us
    pallas_call x2, Pallas kernels, down_project(): pl.pallas_call(functools.partial(down_kernel, groups), name=name, grid=(8...  14.5 us
    ppermute x13, starting transfers between devices, over_y(): return lax.ppermute(v, 'seq', [(i, i ^ 2) for i in range(4)])  14.1 us
    pallas_call x4, Pallas kernels, up_project(): pl.pallas_call(functools.partial(up_kernel, carry is None, features, len(...  13.2 us
  transfers between devices with their start and end apart: 38, of which 24 were waited for; matrix products, arithmetic and copies ran while one was open for 0% of the time, Pallas kernels for 17%

commit v1 on v0

--- a/solution.py
+++ b/solution.py
@@ -202,13 +202,28 @@
         other_ref[k] = dot(sel_ref[2 * k + 1], stream).astype(BF16)
 
 
-def up_kernel(first, features, after, me, *refs):
-    own, rx, ry, even, odd, gain, wg, wu = refs[:8]
+def up_kernel(first, features, after, group, me, *refs):
+    own, rx, ry, even, odd, gain, w_gate, w_up = refs[:8]
     carry = () if first else refs[8:11]
-    rest = refs[(8 if first else 11) + after :]
+    rest, (held_gate, held_up, sems) = refs[(8 if first else 11) + after : -3], refs[-3:]
     sums = rest[2:5] if features else rest
     step = pl.program_id(0)
-    steps = pl.num_programs(0)
+    steps = held_gate.shape[0]
+    tile = held_gate.shape[1]
+
+    def loads(k):
+        source = me[0] ^ (2 * group + k // (steps // 2))
+        part = pl.ds(pl.multiple_of(k % (steps // 2) * tile, tile), tile)
+        return [
+            pltpu.make_async_copy(w.at[source, part, :], held.at[k], sems.at[side, k])
+            for side, (w, held) in enumerate(((w_gate, held_gate), (w_up, held_up)))
+        ]
+
+    @pl.when(step == 0)
+    def _():
+        for k in range(steps):
+            for load in loads(k):
+                load.start()
 
     if first or features:
 
@@ -220,12 +235,14 @@
     gate, up, square = sums
     slots = own.shape[1]
     rows = [r[0].astype(F32) for r in (own, rx, ry)]
-    rows.append(jnp.where(step == 0, even[0].astype(F32), odd[0].astype(F32)))
+    rows.append(jnp.where(step < steps // 2, even[0].astype(F32), odd[0].astype(F32)))
     rows = jnp.concatenate(rows, axis=0)
     square[...] += jnp.broadcast_to(jnp.sum(rows * rows, axis=1, keepdims=True), square.shape)
     scaled = (rows * gain[0]).astype(BF16)
-    gate[...] += dot(scaled, wg[0])
-    up[...] += dot(scaled, wu[0])
+    for load in loads(step):
+        load.wait()
+    gate[...] += dot(scaled, held_gate[step])
+    up[...] += dot(scaled, held_up[step])
 
     if features:
         outs, stages = rest[:2], rest[5:]
@@ -248,18 +265,25 @@
 
 def up_project(group, last, me, near, far, gain, w_gate, w_up, carry, after=()):
     slots, part = near[0][0].shape[1:]
+    cut = 2
+    tile = part // cut
     hidden = w_gate.shape[2]
     total = 4 * slots
-    source = lambda i, me: me[0] ^ (2 * group + i)
+    source = lambda i, me: me[0] ^ (2 * group + i // cut)
     rows = [
-        pl.BlockSpec((1, slots, part), lambda i, me, start=start: (start + i, 0, 0))
+        pl.BlockSpec((1, slots, tile), lambda i, me, start=start: (start + i // cut, 0, i % cut))
         for _, start in near
     ] + [
-        pl.BlockSpec((1, slots, part), lambda i, me, start=start: (start, 0, 0)) for _, start in far
+        pl.BlockSpec((1, slots, tile), lambda i, me, start=start: (start, 0, i % cut))
+        for _, start in far
     ]
-    weight = pl.BlockSpec((1, part, hidden), lambda i, me: (source(i, me), 0, 0))
+    weight = pl.BlockSpec(memory_space=pltpu.HBM)
     in_place = pl.BlockSpec(memory_space=pltpu.VMEM)
-    specs = rows + [pl.BlockSpec((1, 1, part), lambda i, me: (source(i, me), 0, 0)), weight, weight]
+    specs = rows + [
+        pl.BlockSpec((1, 1, tile), lambda i, me: (source(i, me), 0, i % cut)),
+        weight,
+        weight,
+    ]
     sums = [
         jax.ShapeDtypeStruct((total, hidden), F32),
         jax.ShapeDtypeStruct((total, hidden), F32),
@@ -277,15 +301,17 @@
     scratch += [pltpu.VMEM((n, hidden), F32) for n in sizes]
     features = gain.shape[0] * part if last else 0
     return pl.pallas_call(
-        functools.partial(up_kernel, carry is None, features, len(after)),
+        functools.partial(up_kernel, carry is None, features, len(after), group),
         name=f"up_{group}",
         out_shape=outs,
         grid_spec=pltpu.PrefetchScalarGridSpec(
             num_scalar_prefetch=1,
-            grid=(2,),
+            grid=(2 * cut,),
             in_specs=specs,
             out_specs=[in_place] * len(outs),
-            scratch_shapes=scratch if last else [],
+            scratch_shapes=(scratch if last else [])
+            + [pltpu.VMEM((2 * cut, tile, hidden), BF16)] * 2
+            + [pltpu.SemaphoreType.DMA((2, 2 * cut))],
         ),
         input_output_aliases=aliases,
         compiler_params=pltpu.CompilerParams(vmem_limit_bytes=48 * MIB),
@@ -298,9 +324,21 @@
 
 
 def down_kernel(groups, act_ref, w_ref, *refs):
-    outs, spare = refs[:-1], refs[-1]
+    outs, (spare, held, sems) = refs[:-3], refs[-3:]
     step = pl.program_id(0)
-    part = dot(act_ref[...], w_ref[...])
+    steps, _, tile = held.shape
+
+    def load(k):
+        columns = pl.ds(pl.multiple_of(k * tile, tile), tile)
+        return pltpu.make_async_copy(w_ref.at[:, columns], held.at[k], sems.at[k])
+
+    @pl.when(step == 0)
+    def _():
+        for k in range(steps):
+            load(k).start()
+
+    load(step).wait()
+    part = dot(act_ref[...], held[step])
     ninths = part.shape[0] // 9
     main = part.shape[0] - ninths
     shards = ninths // (2 * groups)
@@ -332,7 +370,7 @@
             main:, lanes * 128 : (lanes + 1) * 128
         ]
 
-    @pl.when(step == pl.num_programs(0) - 1)
+    @pl.when(step == steps - 1)
     def _():
         for shard in range(shards):
             for group in range(groups):
@@ -361,22 +399,32 @@
         out_shape=outs,
         in_specs=[
             pl.BlockSpec(memory_space=pltpu.VMEM),
-            pl.BlockSpec((hidden, tile), lambda i: (0, i)),
+            pl.BlockSpec(memory_space=pltpu.HBM),
         ],
         out_specs=[pl.BlockSpec(memory_space=pltpu.VMEM)] * len(outs),
-        scratch_shapes=[pltpu.VMEM((tile // 128, 8 * total // 9, 128), F32)],
+        scratch_shapes=[
+            pltpu.VMEM((tile // 128, 8 * total // 9, 128), F32),
+            pltpu.VMEM((8, hidden, tile), BF16),
+            pltpu.SemaphoreType.DMA((8,)),
+        ],
         compiler_params=pltpu.CompilerParams(vmem_limit_bytes=48 * MIB),
         cost_estimate=NO_COST,
     )(active, w_down)
 
 
-def pair_kernel(same, other, *outs):
-    groups = len(outs) // 2
-    owned = outs[groups].shape[1]
-    for k in range(groups):
-        for side, rows in enumerate((same, other)):
-            outs[k][side] = rows[k, owned:, :]
-            outs[groups + k][side] = rows[k, 0:owned, :]
+def pair_kernel(same, other, own, own_stream, near, far, last, last_stream):
+    owned = own_stream.shape[1]
+    for side, rows in enumerate((same, other)):
+        own_stream[side], own[side] = rows[0, 0:owned, :], rows[0, owned:, :]
+        near[side], far[side] = rows[1], rows[2]
+        last_stream[side], last[side] = rows[3, 0:owned, :], rows[3, owned:, :]
+
+
+def near_kernel(arrived, far, rows, stream, far_out):
+    owned = stream.shape[1]
+    for side in range(2):
+        stream[side], rows[side] = arrived[side, 0:owned, :], arrived[side, owned:, :]
+        far_out[side] = far[side]
 
 
 def second_kernel(*refs):
@@ -387,11 +435,6 @@
             out[h, k] = jnp.concatenate(pair, axis=0).astype(BF16)
 
 
-def holds_kernel(*refs):
-    for source, target in zip(refs[: len(refs) // 2], refs[len(refs) // 2 :]):
-        target[...] = source[...]
-
-
 def hold_kernel(a, out):
     out[...] = a[...]
 
@@ -400,8 +443,13 @@
     out_x[0], out_y[0] = ry[1], rx[0]
 
 
-def join_message_kernel(own, rx, ry, out_x, out_y):
-    out_x[0:2], out_y[0:2] = own[...], own[...]
+def join_message_kernel(own, rx, ry, out_x, out_y, *parts):
+    owned = own.shape[1] - out_x.shape[1]
+    for side in range(2):
+        rows = own[side, owned:, :]
+        out_x[side], out_y[side] = rows, rows
+        if parts:
+            parts[0][side], parts[1][side] = rows, own[side, 0:owned, :]
     out_x[2], out_y[2] = ry[1], rx[0]
 
 
@@ -580,14 +628,19 @@
     gain = norm_gain.reshape(owners, 1, channels)
     wg = w_gate.reshape(owners, channels, w_gate.shape[2])
     wu = w_up.reshape(owners, channels, w_up.shape[2])
-    sets = list(block_call(
+    expert_rows = jax.ShapeDtypeStruct((2, slots, channels), BF16)
+    stream_rows = jax.ShapeDtypeStruct((2, rows, channels), BF16)
+    both_rows = jax.ShapeDtypeStruct((2, rows + slots, channels), BF16)
+    first, stream0, near, far, farthest, stream3 = block_call(
         pair_kernel,
-        [jax.ShapeDtypeStruct((2, slots, channels), BF16)] * groups
-        + [jax.ShapeDtypeStruct((2, rows, channels), BF16)] * groups,
+        [expert_rows, stream_rows, both_rows, both_rows, expert_rows, stream_rows],
         0,
         (same, along(other, 1)),
-    ))
-    sets, streams = sets[:groups], sets[groups:]
+    )
+    gain = norm_gain.reshape(owners, 1, channels)
+    wg = w_gate.reshape(owners, channels, w_gate.shape[2])
+    wu = w_up.reshape(owners, channels, w_up.shape[2])
+
     def hold(v, after, name):
         return block_call(
             hold_kernel, [jax.ShapeDtypeStruct(v.shape, BF16)], 0, (v,), after=after, name=name
@@ -598,23 +651,29 @@
         return up_project(group, last, self_id, near, far, gain, wg, wu, carry, after)
 
     def message(count):
-        return [jax.ShapeDtypeStruct((count,) + sets[0].shape[1:], BF16)] * 2
-
-    near, far, farthest = along(sets[1], 2), along(sets[2], 4), sets[3]
-    rx0, ry0 = over_x(sets[0]), over_y(sets[0])
+        return [jax.ShapeDtypeStruct((count, slots, channels), BF16)] * 2
+
+    near = along(near, 2)
+    rx0, ry0 = over_x(first), over_y(first)
     to_x, to_y = block_call(half_message_kernel, message(1), 0, (rx0, ry0), name="half_0")
     fx0, fy0 = over_x(to_x), over_y(to_y)
-    near = hold(near, (to_x,), "hold_near")
+    near, stream1, far = block_call(
+        near_kernel, [expert_rows, stream_rows, both_rows], 0, (near, far), after=(to_x,)
+    )
+    far = along(far, 4)
+    rx1, ry1 = over_x(near), over_y(near)
     farthest_held = hold(farthest, (far,), "hold_farthest")
     farthest = along(farthest_held, 6)
-    rx1, ry1 = over_x(near), over_y(near)
-    to_x, to_y = block_call(
-        join_message_kernel, message(3), 0, (far, rx1, ry1), after=(fx0, fy0, farthest_held), name="join_2"
+    to_x, to_y, far, stream2 = block_call(
+        join_message_kernel,
+        message(3) + [expert_rows, stream_rows],
+        0,
+        (far, rx1, ry1),
+        after=(fx0, fy0, farthest_held),
+        name="join_2",
     )
     rx2, ry2 = over_x(to_x), over_y(to_y)
-    carry = project(
-        0, [(sets[0], 0), (rx0, 0), (ry0, 0)], [(fy0, 0), (fx0, 0)], None
-    )
+    carry = project(0, [(first, 0), (rx0, 0), (ry0, 0)], [(fy0, 0), (fx0, 0)], None)
     to_x, to_y = block_call(
         join_message_kernel, message(3), 0, (farthest, rx2, ry2), after=(carry[2],), name="join_3"
     )
@@ -624,16 +683,9 @@
         half_message_kernel, message(1), 0, (rx3, ry3), after=(carry[2],), name="half_3"
     )
     fx3, fy3 = over_x(to_x), over_y(to_y)
-    held = block_call(
-        holds_kernel,
-        [jax.ShapeDtypeStruct(v.shape, BF16) for v in streams[1:]],
-        0,
-        streams[1:],
-        after=(to_x,),
-        name="hold_streams",
-    )
-    streams[1:] = [along(held[g - 1], 2 * g) for g in range(1, groups)]
-    carry = project(2, [(far, 0), (rx2, 0), (ry2, 0)], [(ry3, 2), (rx3, 2)], carry, held[:1])
+    held = hold(stream3, (to_x,), "hold_stream")
+    streams = [stream0, stream1, stream2, along(held, 6)]
+    carry = project(2, [(far, 0), (rx2, 0), (ry2, 0)], [(ry3, 2), (rx3, 2)], carry, (held,))
     active_far, active = project(
         3, [(farthest, 0), (rx3, 0), (ry3, 0)], [(fy3, 0), (fx3, 0)], carry
     )
@@ -667,7 +719,7 @@
 
     through_x, through_y = over_x(sent[2]), over_y(sent[3])
     x2, y2, x3, y3, next_x, next_y = relay(
-        "relay_far", through_x, through_y, 2, (sent[0], sent[1]), streams[1:]
+        "relay_far", through_x, through_y, 2, (sent[0], sent[1]), streams[3:]
     )
     rx3, ry3 = over_x(x3), over_y(y3)
     through_x, through_y = over_x(next_x), over_y(next_y)

time: 158 us -> 164 us (1.038)
  waiting for transfers between devices: 55.6 us -> 60 us
  starting transfers between devices: 51.5 us -> 55 us
  Pallas kernels: 42.3 us -> 40.5 us
    ppermute x11 -> x9, waiting for transfers between devices: 20.8 us -> 29.9 us  [along(): return lax.ppermute(v, 'exp', [(i, i ^ mask) for i in range(owners)])]
    ppermute x13, waiting for transfers between devices: 18 us -> 11.4 us  [over_y(): return lax.ppermute(v, 'seq', [(i, i ^ 2) for i in range(4)])]
    pallas_call x2, Pallas kernels: 14.5 us -> 9.3 us  [down_project(): pl.pallas_call(functools.partial(down_kernel, groups), name=name, grid=(8...]
    pallas_call x4, Pallas kernels: 13.2 us -> 16.6 us  [up_project(): pl.pallas_call(functools.partial(up_kernel, carry is None, features, len(...]
    ppermute x13, starting transfers between devices: 14.1 us -> 16.6 us  [over_y(): return lax.ppermute(v, 'seq', [(i, i ^ 2) for i in range(4)])]
    ppermute x13, starting transfers between devices: 12.7 us -> 14.9 us  [over_x(): return lax.ppermute(v, 'seq', [(i, i ^ 1) for i in range(4)])]
    ppermute x13, waiting for transfers between devices: 16.8 us -> 18.7 us  [over_x(): return lax.ppermute(v, 'seq', [(i, i ^ 1) for i in range(4)])]
    ppermute x11 -> x9, starting transfers between devices: 18.3 us -> 17.2 us  [along(): return lax.ppermute(v, 'exp', [(i, i ^ mask) for i in range(owners)])]
  transfers between devices with their start and end apart: 38 -> 36, of which waited for: 24 -> 18; matrix products, arithmetic and copies ran while one was open for 0% -> 0% of each run, Pallas kernels for 17% -> 17%
where the time goes in v1:
time: 164 us; the launch traced here: 163 us
  waiting for transfers between devices  60 us (37%)
  starting transfers between devices  55 us (34%)
  Pallas kernels  40.5 us (25%)
  local copies, waits for them, and re-layouts  7.61 us (5%)
    ppermute x9, waiting for transfers between devices, along(): return lax.ppermute(v, 'exp', [(i, i ^ mask) for i in range(owners)])  29.9 us
    ppermute x13, waiting for transfers between devices, over_x(): return lax.ppermute(v, 'seq', [(i, i ^ 1) for i in range(4)])  18.7 us
    ppermute x9, starting transfers between devices, along(): return lax.ppermute(v, 'exp', [(i, i ^ mask) for i in range(owners)])  17.2 us
    pallas_call x4, Pallas kernels, up_project(): pl.pallas_call(functools.partial(up_kernel, carry is None, features, len(...  16.6 us
    ppermute x13, starting transfers between devices, over_y(): return lax.ppermute(v, 'seq', [(i, i ^ 2) for i in range(4)])  16.6 us
    ppermute x13, starting transfers between devices, over_x(): return lax.ppermute(v, 'seq', [(i, i ^ 1) for i in range(4)])  14.9 us
    pallas_call x22, Pallas kernels, block_call(): pl.pallas_call(kernel, name=name or getattr(body, 'func', body).__name__,...  14.7 us
    ppermute x13, waiting for transfers between devices, over_y(): return lax.ppermute(v, 'seq', [(i, i ^ 2) for i in range(4)])  11.4 us
  transfers between devices with their start and end apart: 36, of which 18 were waited for; matrix products, arithmetic and copies ran while one was open for 0% of the time, Pallas kernels for 17%

profile of v1, /device:TPU:0, one launch (start us, length us, event | category | flops | bytes accessed | tf_op | source)
XLA Modules:
  0.0 163.4 jit_solution(16588737084959931685)
XLA Ops:
  0.0 1.0 copy-done.3
  1.0 0.7 copy-done.8
  1.7 1.0 pack_kernel.1
  2.7 6.3 %all-to-all-start = ((bf16[8,32,1152]{2,1,0:T(8,128)(2,1)}), bf16[8,32,1152]{2,1,0:T(8,128)(2,1)S(1)}, u32[]{:S(2)}, u32[]{:S(2)}) async-start(bf16[8,32,1152]{2,1,0:T(8,128)(2,1)} %pack_kernel.1), calls=%async_computation | async-start | bytes 1179648 | tf_op jit(solution)/shard_map/all_to_all | solution.py:577
  9.1 4.1 %state_kernel.1 = (bf16[144,1024]{1,0:T(8,128)(2,1)}, bf16[128,1024]{1,0:T(8,128)(2,1)}) custom-call(s32[1]{0:T(128)} %bitcast.3.refs_0_, bf16[256,1024]{1,0:T(8,128)(2,1)} %refs_1_.5, bf16[256,128]{1,0:T(8,128)(2,1)} %refs_2_.3, f32[16,256]{1,0:T(8,128)} %bitcast.30, f32[1,16]{1,0:T(1,128)} %bitcast.32, f32[1024,128]{1,0:T(8,128)} %bitcast.29), custom_call_target="tpu_custom_call" | custom-call | tf_op jit(solution)/shard_map/state_kernel/pallas_call | solution.py:39
  13.2 1.6 collective-permute-start
  14.8 4.7 %intra_kernel.1 = (f32[256,1024]{1,0:T(8,128)}, f32[256,1024]{1,0:T(8,128)}, f32[8,128]{1,0:T(8,128)}) custom-call(bf16[256,1024]{1,0:T(8,128)(2,1)} %refs_1_.5, bf16[256,1024]{1,0:T(8,128)(2,1)} %refs_1_.4, bf16[256,128]{1,0:T(8,128)(2,1)} %refs_2_.3, bf16[256,128]{1,0:T(8,128)(2,1)} %refs_4_.1, f32[16,256]{1,0:T(8,128)} %bitcast.31, f32[1,16]{1,0:T(1,128)} %bitcast.33, ...), custom_call_target="tpu_custom_call" | custom-call | tf_op jit(solution)/shard_map/intra_kernel/pallas_call | solution.py:39
  19.5 3.4 %collective-permute-done.refs_2_.refs_5_ = bf16[144,1024]{1,0:T(8,128)(2,1)S(1)} collective-permute-done((bf16[144,1024]{1,0:T(8,128)(2,1)}, bf16[144,1024]{1,0:T(8,128)(2,1)S(1)}, u32[]{:S(2)}, u32[]{:S(2)}) %collective-permute-start) | collective-permute-done | bytes 294944 | tf_op jit(solution)/shard_map/ppermute | solution.py:558
  22.9 1.0 copy-done.4
  24.7 1.6 collective-permute-start.1
  26.3 1.2 copy-done
  27.5 1.2 copy-done.1
  28.7 0.9 copy-done.5
  29.7 0.8 copy-done.6
  30.9 1.8 %collective-permute-done.1.refs_6_ = bf16[128,1024]{1,0:T(8,128)(2,1)S(1)} collective-permute-done((bf16[128,1024]{1,0:T(8,128)(2,1)S(1)}, bf16[128,1024]{1,0:T(8,128)(2,1)S(1)}, u32[]{:S(2)}, u32[]{:S(2)}) %collective-permute-start.1) | collective-permute-done | bytes 262176 | tf_op jit(solution)/shard_map/ppermute | solution.py:561
  32.7 1.2 stream_kernel.1
  33.9 2.4 %collective-permute-done.2.refs_1_ = bf16[4,104,1024]{2,1,0:T(8,128)(2,1)S(1)} collective-permute-done((bf16[4,104,1024]{2,1,0:T(8,128)(2,1)S(1)}, bf16[4,104,1024]{2,1,0:T(8,128)(2,1)S(1)}, u32[]{:S(2)}, u32[]{:S(2)}) %collective-permute-start.2) | collective-permute-done | bytes 852000 | tf_op jit(solution)/shard_map/ppermute | solution.py:564
  36.4 1.3 collective-permute-start.3
  37.7 1.5 collective-permute-start.5
  39.3 1.5 collective-permute-start.4
  40.8 5.8 %collective-permute-done.5.refs_1_.refs_2_ = bf16[2,72,1024]{2,1,0:T(8,128)(2,1)S(1)} collective-permute-done((bf16[2,72,1024]{2,1,0:T(8,128)(2,1)S(1)}, bf16[2,72,1024]{2,1,0:T(8,128)(2,1)S(1)}, u32[]{:S(2)}, u32[]{:S(2)}) %collective-permute-start.5) | collective-permute-done | bytes 294944 | tf_op jit(solution)/shard_map/ppermute | solution.py:561
  46.5 1.2 collective-permute-done.4.refs_0_.refs_1_
  48.4 2.2 %collective-permute-start.6 = (bf16[2,104,1024]{2,1,0:T(8,128)(2,1)S(1)}, bf16[2,104,1024]{2,1,0:T(8,128)(2,1)S(1)}, u32[]{:S(2)}, u32[]{:S(2)}) collective-permute-start(bf16[2,104,1024]{2,1,0:T(8,128)(2,1)S(1)} %get-tuple-element.96), channel_id=1, source_target_pairs={{0,4},{1,5},{2,6},{3,7},{4,0},{5,1},{6,2},{7,3},{8,12},{9,13},{10,... | collective-permute-start | bytes 1277960 | tf_op jit(solution)/shard_map/ppermute | solution.py:564
  50.6 1.5 collective-permute-start.9
  52.1 1.5 collective-permute-start.8
  54.7 14.8 %collective-permute-done.6.refs_1_.refs_0_ = bf16[2,104,1024]{2,1,0:T(8,128)(2,1)S(1)} collective-permute-done((bf16[2,104,1024]{2,1,0:T(8,128)(2,1)S(1)}, bf16[2,104,1024]{2,1,0:T(8,128)(2,1)S(1)}, u32[]{:S(2)}, u32[]{:S(2)}) %collective-permute-start.6) | collective-permute-done | bytes 426016 | tf_op jit(solution)/shard_map/ppermute | solution.py:564
  69.7 1.6 collective-permute-start.12
  71.2 1.5 collective-permute-start.13
  72.8 3.1 %collective-permute-start.7 = (bf16[2,72,1024]{2,1,0:T(8,128)(2,1)S(1)}, bf16[2,72,1024]{2,1,0:T(8,128)(2,1)S(1)}, u32[]{:S(2)}, u32[]{:S(2)}) collective-permute-start(bf16[2,72,1024]{2,1,0:T(8,128)(2,1)S(1)} %hold_farthest.1.refs_5_), channel_id=1, source_target_pairs={{0,6},{1,7},{2,4},{3,5},{4,2},{5,3},{6,0},{7,1},{8,14},{9,15},{10,... | collective-permute-start | bytes 884744 | tf_op jit(solution)/shard_map/ppermute | solution.py:564
  75.8 4.1 %up_0.1 = (f32[288,512]{1,0:T(8,128)S(1)}, f32[288,512]{1,0:T(8,128)S(1)}, f32[288,128]{1,0:T(8,128)S(1)}) custom-call(s32[1]{0:T(128)} %bitcast.refs_0_.me, bf16[2,72,1024]{2,1,0:T(8,128)(2,1)S(1)} %get-tuple-element.94.refs_0_, bf16[2,72,1024]{2,1,0:T(8,128)(2,1)S(1)} %collective-permute-done.4.refs_0_.refs_1_, ...), custom_call_target="tpu_custom_call" | custom-call | tf_op jit(solution)/shard_map/up_0/pallas_call | solution.py:303
  79.9 2.7 %collective-permute-done.7.refs_0_ = bf16[2,72,1024]{2,1,0:T(8,128)(2,1)S(1)} collective-permute-done((bf16[2,72,1024]{2,1,0:T(8,128)(2,1)S(1)}, bf16[2,72,1024]{2,1,0:T(8,128)(2,1)S(1)}, u32[]{:S(2)}, u32[]{:S(2)}) %collective-permute-start.7) | collective-permute-done | bytes 294944 | tf_op jit(solution)/shard_map/ppermute | solution.py:564
  83.2 1.2 collective-permute-start.15
  84.5 4.1 %up_1.1 = (f32[288,512]{1,0:T(8,128)S(1)}, f32[288,512]{1,0:T(8,128)S(1)}, f32[288,128]{1,0:T(8,128)S(1)}) custom-call(s32[1]{0:T(128)} %bitcast.refs_0_.me, bf16[2,72,1024]{2,1,0:T(8,128)(2,1)S(1)} %get-tuple-element.97.refs_0_, ...), custom_call_target="tpu_custom_call", output_to_operand_aliasing={{0}: (9, {}), {1}: (10, {}), {2}: (11, {})} | custom-call | tf_op jit(solution)/shard_map/up_1/pallas_call | solution.py:303
  88.5 4.3 %collective-permute-done.14.refs_0_.refs_4_.refs_1_ = bf16[3,72,1024]{2,1,0:T(8,128)(2,1)S(1)} collective-permute-done((bf16[3,72,1024]{2,1,0:T(8,128)(2,1)S(1)}, bf16[3,72,1024]{2,1,0:T(8,128)(2,1)S(1)}, u32[]{:S(2)}, u32[]{:S(2)}) %collective-permute-start.14) | collective-permute-done | bytes 442400 | tf_op jit(solution)/shard_map/ppermute | solution.py:558
  92.8 0.7 collective-permute-done.15.refs_1_.refs_3_.refs_2_
  93.5 1.3 collective-permute-start.16
  94.8 1.5 collective-permute-start.17
  96.3 4.1 %up_2.1 = (f32[288,512]{1,0:T(8,128)S(1)}, f32[288,512]{1,0:T(8,128)S(1)}, f32[288,128]{1,0:T(8,128)S(1)}) custom-call(s32[1]{0:T(128)} %bitcast.refs_0_.me, bf16[2,72,1024]{2,1,0:T(8,128)(2,1)S(1)} %get-tuple-element.109.refs_0_, ...), custom_call_target="tpu_custom_call", output_to_operand_aliasing={{0}: (9, {}), {1}: (10, {}), {2}: (11, {})} | custom-call | tf_op jit(solution)/shard_map/up_2/pallas_call | solution.py:303
  100.4 4.4 %up_3.1 = (bf16[72,512]{1,0:T(8,128)(2,1)S(1)}, bf16[216,512]{1,0:T(8,128)(2,1)S(1)}) custom-call(s32[1]{0:T(128)} %bitcast.refs_0_.me, bf16[2,72,1024]{2,1,0:T(8,128)(2,1)S(1)} %collective-permute-done.7.refs_0_, bf16[3,72,1024]{2,1,0:T(8,128)(2,1)S(1)} %collective-permute-done.14.refs_0_.refs_4_.refs_1_, ...), custom_call_target="tpu_custom_call" | custom-call | tf_op jit(solution)/shard_map/up_3/pallas_call | solution.py:303
  104.8 4.2 %down_through.1 = (bf16[9,16,1024]{2,1,0:T(8,128)(2,1)S(1)}, bf16[9,16,1024]{2,1,0:T(8,128)(2,1)S(1)}, bf16[9,16,1024]{2,1,0:T(8,128)(2,1)S(1)}, bf16[9,16,1024]{2,1,0:T(8,128)(2,1)S(1)}) custom-call(bf16[72,512]{1,0:T(8,128)(2,1)S(1)} %get-tuple-element.120.act_ref, bf16[512,8192]{1,0:T(8,128)(2,1)} %bitcast.27), custom_call_target="tpu_custom_call" | custom-call | tf_op jit(solution)/shard_map/down_through/pallas_call | solution.py:395
  109.0 1.0 collective-permute-start.18
  110.0 0.8 collective-permute-start.19
  110.8 4.0 %collective-permute-start.20 = (bf16[2,32,1024]{2,1,0:T(8,128)(2,1)S(1)}, bf16[2,32,1024]{2,1,0:T(8,128)(2,1)S(1)}, u32[]{:S(2)}, u32[]{:S(2)}) collective-permute-start(bf16[2,32,1024]{2,1,0:T(8,128)(2,1)S(1)} %hold_stream.1.refs_11_), channel_id=1, source_target_pairs={{0,6},{1,7},{2,4},{3,5},{4,2},{5,3},{6,0},{7,1},{8,14},{9,15},{10,... | collective-permute-start | bytes 393224 | tf_op jit(solution)/shard_map/ppermute | solution.py:564
  114.7 5.1 %down_rest.1 = (bf16[9,16,1024]{2,1,0:T(8,128)(2,1)S(1)}, bf16[9,16,1024]{2,1,0:T(8,128)(2,1)S(1)}, bf16[9,16,1024]{2,1,0:T(8,128)(2,1)S(1)}, bf16[9,16,1024]{2,...) custom-call(bf16[216,512]{1,0:T(8,128)(2,1)S(1)} %get-tuple-element., ...), custom_call_target="tpu_custom_call" | custom-call | tf_op jit(solution)/shard_map/down_rest/pallas_call | solution.py:395
  120.1 1.1 collective-permute-start.21
  121.2 1.5 collective-permute-start.22
  122.7 0.9 collective-permute-start.25
  124.2 5.9 %collective-permute-done.21.refs_1_ = bf16[9,16,1024]{2,1,0:T(8,128)(2,1)S(1)} collective-permute-done((bf16[9,16,1024]{2,1,0:T(8,128)(2,1)S(1)}, bf16[9,16,1024]{2,1,0:T(8,128)(2,1)S(1)}, u32[]{:S(2)}, u32[]{:S(2)}) %collective-permute-start.21) | collective-permute-done | bytes 294944 | tf_op jit(solution)/shard_map/ppermute | solution.py:558
  130.1 1.1 collective-permute-done.22.refs_2_
  131.3 1.0 collective-permute-start.23
  132.3 1.5 collective-permute-start.24
  133.8 1.3 collective-permute-start.31
  135.1 1.3 collective-permute-done.25.refs_0_
  136.4 1.1 collective-permute-done.26.refs_1_
  137.6 1.0 collective-permute-start.29
  138.7 1.5 collective-permute-start.30
  140.2 2.6 %collective-permute-done.23.refs_1_ = bf16[9,16,1024]{2,1,0:T(8,128)(2,1)S(1)} collective-permute-done((bf16[9,16,1024]{2,1,0:T(8,128)(2,1)S(1)}, bf16[9,16,1024]{2,1,0:T(8,128)(2,1)S(1)}, u32[]{:S(2)}, u32[]{:S(2)}) %collective-permute-start.23) | collective-permute-done | bytes 294944 | tf_op jit(solution)/shard_map/ppermute | solution.py:558
  142.7 1.1 collective-permute-done.24.refs_2_
  143.9 1.0 collective-permute-start.27
  145.0 1.5 collective-permute-start.28
  146.5 5.0 %collective-permute-start.33 = (bf16[9,16,1024]{2,1,0:T(8,128)(2,1)S(1)}, bf16[9,16,1024]{2,1,0:T(8,128)(2,1)S(1)}, u32[]{:S(2)}, u32[]{:S(2)}) collective-permute-start(bf16[9,16,1024]{2,1,0:T(8,128)(2,1)S(1)} %get-tuple-element.149), channel_id=1, source_target_pairs={{0,4},{1,5},{2,6},{3,7},{4,0},{5,1},{6,2},{7,3},{8,12},{9,13},{10,... | collective-permute-start | bytes 884744 | tf_op jit(solution)/shard_map/ppermute | solution.py:564
  151.9 7.5 %collective-permute-done.33.refs_2_.refs_6_ = bf16[9,16,1024]{2,1,0:T(8,128)(2,1)S(1)} collective-permute-done((bf16[9,16,1024]{2,1,0:T(8,128)(2,1)S(1)}, bf16[9,16,1024]{2,1,0:T(8,128)(2,1)S(1)}, u32[]{:S(2)}, u32[]{:S(2)}) %collective-permute-start.33) | collective-permute-done | bytes 294944 | tf_op jit(solution)/shard_map/ppermute | solution.py:564
  159.5 2.0 %collective-permute-done.34.refs_3_ = bf16[2,9,16,1024]{3,2,1,0:T(8,128)(2,1)S(1)} collective-permute-done((bf16[2,9,16,1024]{3,2,1,0:T(8,128)(2,1)S(1)}, bf16[2,9,16,1024]{3,2,1,0:T(8,128)(2,1)S(1)}, u32[]{:S(2)}, u32[]{:S(2)}) %collective-permute-start.34) | collective-permute-done | bytes 589856 | tf_op jit(solution)/shard_map/ppermute | solution.py:564
  161.5 1.9 %mix_kernel.1 = bf16[32,8192]{1,0:T(8,128)(2,1)} custom-call(s32[1]{0:T(128)} %bitcast.refs_0_.me, s32[2,32]{1,0:T(2,128)S(1)} %bitcast.17, f32[2,32]{1,0:T(2,128)S(1)} %bitcast.18, bf16[2,9,16,1024]{3,2,1,0:T(8,128)(2,1)S(1)} %collective-permute-done.34.refs_3_, bf16[9,16,1024]{2,1,0:T(8,128)(2,1)S(1)} %finish_0.1.refs_0_.refs_4_, ...), custom_call_target="tpu_custom_call" | custom-call | tf_op jit(solution)/shard_map/mix_kernel/pallas_call | solution.py:39
  (58 shorter events, 5.5 us)
Async XLA Ops:
  0.0 1.0 copy-start.3
  1.0 0.7 copy-start.8
  2.7 23.5 %all-to-all-start = ((bf16[8,32,1152]{2,1,0:T(8,128)(2,1)}), bf16[8,32,1152]{2,1,0:T(8,128)(2,1)S(1)}, u32[]{:S(2)}, u32[]{:S(2)}) async-start(bf16[8,32,1152]{2,1,0:T(8,128)(2,1)} %pack_kernel.1), calls=%async_computation | async-start | bytes 1179648 | tf_op jit(solution)/shard_map/all_to_all | solution.py:577
  9.1 66.7 %copy-start.2 = (f32[8192]{0:T(1024)S(1)}, f32[8192]{0:T(1024)}, u32[]{:S(2)}) copy-start(f32[8192]{0:T(1024)} %param.24) | copy-start | bytes 98308
  13.2 9.7 %collective-permute-start = (bf16[144,1024]{1,0:T(8,128)(2,1)}, bf16[144,1024]{1,0:T(8,128)(2,1)S(1)}, u32[]{:S(2)}, u32[]{:S(2)}) collective-permute-start(bf16[144,1024]{1,0:T(8,128)(2,1)} %get-tuple-element.82.refs_1_), channel_id=1, source_target_pairs={{0,8},{8,0},{16,24},{24,16},{1,9},{9,1},{17,25},{25,17},{2,10},{10... | collective-permute-start | bytes 884744 | tf_op jit(solution)/shard_map/ppermute | solution.py:558
  22.9 1.0 copy-start.4
  23.9 0.7 copy-start.7
  24.7 8.0 %collective-permute-start.1 = (bf16[128,1024]{1,0:T(8,128)(2,1)S(1)}, bf16[128,1024]{1,0:T(8,128)(2,1)S(1)}, u32[]{:S(2)}, u32[]{:S(2)}) collective-permute-start(bf16[128,1024]{1,0:T(8,128)(2,1)S(1)} %join_kernel.1.refs_6_), channel_id=1, source_target_pairs={{0,16},{8,24},{16,0},{24,8},{1,17},{9,25},{17,1},{25,9},{2,18},{10... | collective-permute-start | bytes 786440 | tf_op jit(solution)/shard_map/ppermute | solution.py:561
  26.3 1.2 copy-start
  27.5 1.2 copy-start.1
  28.7 0.9 copy-start.5
  29.7 0.8 copy-start.6
  33.9 2.4 %collective-permute-start.2 = (bf16[4,104,1024]{2,1,0:T(8,128)(2,1)S(1)}, bf16[4,104,1024]{2,1,0:T(8,128)(2,1)S(1)}, u32[]{:S(2)}, u32[]{:S(2)}) collective-permute-start(bf16[4,104,1024]{2,1,0:T(8,128)(2,1)S(1)} %get-tuple-element.90), channel_id=1, source_target_pairs={{0,1},{1,0},{2,3},{3,2},{4,5},{5,4},{6,7},{7,6},{8,9},{9,8},{10,11... | collective-permute-start | bytes 2555912 | tf_op jit(solution)/shard_map/ppermute | solution.py:564
  36.4 11.9 %collective-permute-start.3 = (bf16[2,104,1024]{2,1,0:T(8,128)(2,1)S(1)}, bf16[2,104,1024]{2,1,0:T(8,128)(2,1)S(1)}, u32[]{:S(2)}, u32[]{:S(2)}) collective-permute-start(bf16[2,104,1024]{2,1,0:T(8,128)(2,1)S(1)} %get-tuple-element.92), channel_id=1, source_target_pairs={{0,2},{1,3},{2,0},{3,1},{4,6},{5,7},{6,4},{7,5},{8,10},{9,11},{10,... | collective-permute-start | bytes 1277960 | tf_op jit(solution)/shard_map/ppermute | solution.py:564
  37.7 8.8 %collective-permute-start.5 = (bf16[2,72,1024]{2,1,0:T(8,128)(2,1)S(1)}, bf16[2,72,1024]{2,1,0:T(8,128)(2,1)S(1)}, u32[]{:S(2)}, u32[]{:S(2)}) collective-permute-start(bf16[2,72,1024]{2,1,0:T(8,128)(2,1)S(1)} %get-tuple-element.94.refs_0_), channel_id=1, source_target_pairs={{0,16},{8,24},{16,0},{24,8},{1,17},{9,25},{17,1},{25,9},{2,18},{10... | collective-permute-start | bytes 884744 | tf_op jit(solution)/shard_map/ppermute | solution.py:561
  39.3 8.5 %collective-permute-start.4 = (bf16[2,72,1024]{2,1,0:T(8,128)(2,1)S(1)}, bf16[2,72,1024]{2,1,0:T(8,128)(2,1)S(1)}, u32[]{:S(2)}, u32[]{:S(2)}) collective-permute-start(bf16[2,72,1024]{2,1,0:T(8,128)(2,1)S(1)} %get-tuple-element.94.refs_0_), channel_id=1, source_target_pairs={{0,8},{8,0},{16,24},{24,16},{1,9},{9,1},{17,25},{25,17},{2,10},{10... | collective-permute-start | bytes 884744 | tf_op jit(solution)/shard_map/ppermute | solution.py:558
  48.4 21.1 %collective-permute-start.6 = (bf16[2,104,1024]{2,1,0:T(8,128)(2,1)S(1)}, bf16[2,104,1024]{2,1,0:T(8,128)(2,1)S(1)}, u32[]{:S(2)}, u32[]{:S(2)}) collective-permute-start(bf16[2,104,1024]{2,1,0:T(8,128)(2,1)S(1)} %get-tuple-element.96), channel_id=1, source_target_pairs={{0,4},{1,5},{2,6},{3,7},{4,0},{5,1},{6,2},{7,3},{8,12},{9,13},{10,... | collective-permute-start | bytes 1277960 | tf_op jit(solution)/shard_map/ppermute | solution.py:564
  50.6 18.9 %collective-permute-start.9 = (bf16[2,72,1024]{2,1,0:T(8,128)(2,1)S(1)}, bf16[2,72,1024]{2,1,0:T(8,128)(2,1)S(1)}, u32[]{:S(2)}, u32[]{:S(2)}) collective-permute-start(bf16[2,72,1024]{2,1,0:T(8,128)(2,1)S(1)} %get-tuple-element.97.refs_0_), channel_id=1, source_target_pairs={{0,16},{8,24},{16,0},{24,8},{1,17},{9,25},{17,1},{25,9},{2,18},{10... | collective-permute-start | bytes 884744 | tf_op jit(solution)/shard_map/ppermute | solution.py:561
  52.1 17.4 %collective-permute-start.8 = (bf16[2,72,1024]{2,1,0:T(8,128)(2,1)S(1)}, bf16[2,72,1024]{2,1,0:T(8,128)(2,1)S(1)}, u32[]{:S(2)}, u32[]{:S(2)}) collective-permute-start(bf16[2,72,1024]{2,1,0:T(8,128)(2,1)S(1)} %get-tuple-element.97.refs_0_), channel_id=1, source_target_pairs={{0,8},{8,0},{16,24},{24,16},{1,9},{9,1},{17,25},{25,17},{2,10},{10... | collective-permute-start | bytes 884744 | tf_op jit(solution)/shard_map/ppermute | solution.py:558
  53.6 15.9 %collective-permute-start.11 = (bf16[1,72,1024]{2,1,0:T(8,128)(2,1)S(1)}, bf16[1,72,1024]{2,1,0:T(8,128)(2,1)S(1)}, u32[]{:S(2)}, u32[]{:S(2)}) collective-permute-start(bf16[1,72,1024]{2,1,0:T(8,128)(2,1)S(1)} %get-tuple-element.98), channel_id=1, source_target_pairs={{0,16},{8,24},{16,0},{24,8},{1,17},{9,25},{17,1},{25,9},{2,18},{10... | collective-permute-start | bytes 442376 | tf_op jit(solution)/shard_map/ppermute | solution.py:561
  54.2 15.4 %collective-permute-start.10 = (bf16[1,72,1024]{2,1,0:T(8,128)(2,1)S(1)}, bf16[1,72,1024]{2,1,0:T(8,128)(2,1)S(1)}, u32[]{:S(2)}, u32[]{:S(2)}) collective-permute-start(bf16[1,72,1024]{2,1,0:T(8,128)(2,1)S(1)} %get-tuple-element.95.refs_2_), channel_id=1, source_target_pairs={{0,8},{8,0},{16,24},{24,16},{1,9},{9,1},{17,25},{25,17},{2,10},{10... | collective-permute-start | bytes 442376 | tf_op jit(solution)/shard_map/ppermute | solution.py:558
  69.7 12.9 %collective-permute-start.12 = (bf16[3,72,1024]{2,1,0:T(8,128)(2,1)S(1)}, bf16[3,72,1024]{2,1,0:T(8,128)(2,1)S(1)}, u32[]{:S(2)}, u32[]{:S(2)}) collective-permute-start(bf16[3,72,1024]{2,1,0:T(8,128)(2,1)S(1)} %get-tuple-element.99), channel_id=1, source_target_pairs={{0,8},{8,0},{16,24},{24,16},{1,9},{9,1},{17,25},{25,17},{2,10},{10... | collective-permute-start | bytes 1327112 | tf_op jit(solution)/shard_map/ppermute | solution.py:558
  71.2 11.3 %collective-permute-start.13 = (bf16[3,72,1024]{2,1,0:T(8,128)(2,1)S(1)}, bf16[3,72,1024]{2,1,0:T(8,128)(2,1)S(1)}, u32[]{:S(2)}, u32[]{:S(2)}) collective-permute-start(bf16[3,72,1024]{2,1,0:T(8,128)(2,1)S(1)} %get-tuple-element.100), channel_id=1, source_target_pairs={{0,16},{8,24},{16,0},{24,8},{1,17},{9,25},{17,1},{25,9},{2,18},{10... | collective-permute-start | bytes 1327112 | tf_op jit(solution)/shard_map/ppermute | solution.py:561
  72.8 9.8 %collective-permute-start.7 = (bf16[2,72,1024]{2,1,0:T(8,128)(2,1)S(1)}, bf16[2,72,1024]{2,1,0:T(8,128)(2,1)S(1)}, u32[]{:S(2)}, u32[]{:S(2)}) collective-permute-start(bf16[2,72,1024]{2,1,0:T(8,128)(2,1)S(1)} %hold_farthest.1.refs_5_), channel_id=1, source_target_pairs={{0,6},{1,7},{2,4},{3,5},{4,2},{5,3},{6,0},{7,1},{8,14},{9,15},{10,... | collective-permute-start | bytes 884744 | tf_op jit(solution)/shard_map/ppermute | solution.py:564
  82.6 10.2 %collective-permute-start.14 = (bf16[3,72,1024]{2,1,0:T(8,128)(2,1)S(1)}, bf16[3,72,1024]{2,1,0:T(8,128)(2,1)S(1)}, u32[]{:S(2)}, u32[]{:S(2)}) collective-permute-start(bf16[3,72,1024]{2,1,0:T(8,128)(2,1)S(1)} %get-tuple-element.102), channel_id=1, source_target_pairs={{0,8},{8,0},{16,24},{24,16},{1,9},{9,1},{17,25},{25,17},{2,10},{10... | collective-permute-start | bytes 1327112 | tf_op jit(solution)/shard_map/ppermute | solution.py:558
  83.2 10.2 %collective-permute-start.15 = (bf16[3,72,1024]{2,1,0:T(8,128)(2,1)S(1)}, bf16[3,72,1024]{2,1,0:T(8,128)(2,1)S(1)}, u32[]{:S(2)}, u32[]{:S(2)}) collective-permute-start(bf16[3,72,1024]{2,1,0:T(8,128)(2,1)S(1)} %get-tuple-element.103), channel_id=1, source_target_pairs={{0,16},{8,24},{16,0},{24,8},{1,17},{9,25},{17,1},{25,9},{2,18},{10... | collective-permute-start | bytes 1327112 | tf_op jit(solution)/shard_map/ppermute | solution.py:561
  93.5 6.9 %collective-permute-start.16 = (bf16[1,72,1024]{2,1,0:T(8,128)(2,1)S(1)}, bf16[1,72,1024]{2,1,0:T(8,128)(2,1)S(1)}, u32[]{:S(2)}, u32[]{:S(2)}) collective-permute-start(bf16[1,72,1024]{2,1,0:T(8,128)(2,1)S(1)} %get-tuple-element.107), channel_id=1, source_target_pairs={{0,16},{8,24},{16,0},{24,8},{1,17},{9,25},{17,1},{25,9},{2,18},{10... | collective-permute-start | bytes 442376 | tf_op jit(solution)/shard_map/ppermute | solution.py:561
  94.8 5.6 %collective-permute-start.17 = (bf16[1,72,1024]{2,1,0:T(8,128)(2,1)S(1)}, bf16[1,72,1024]{2,1,0:T(8,128)(2,1)S(1)}, u32[]{:S(2)}, u32[]{:S(2)}) collective-permute-start(bf16[1,72,1024]{2,1,0:T(8,128)(2,1)S(1)} %get-tuple-element.108.refs_1_), channel_id=1, source_target_pairs={{0,8},{8,0},{16,24},{24,16},{1,9},{9,1},{17,25},{25,17},{2,10},{10... | collective-permute-start | bytes 442376 | tf_op jit(solution)/shard_map/ppermute | solution.py:558
  109.0 10.9 %collective-permute-start.18 = (bf16[9,16,1024]{2,1,0:T(8,128)(2,1)S(1)}, bf16[9,16,1024]{2,1,0:T(8,128)(2,1)S(1)}, u32[]{:S(2)}, u32[]{:S(2)}) collective-permute-start(bf16[9,16,1024]{2,1,0:T(8,128)(2,1)S(1)} %get-tuple-element.121), channel_id=1, source_target_pairs={{0,8},{8,0},{16,24},{24,16},{1,9},{9,1},{17,25},{25,17},{2,10},{10... | collective-permute-start | bytes 884744 | tf_op jit(solution)/shard_map/ppermute | solution.py:558
  110.0 9.9 %collective-permute-start.19 = (bf16[9,16,1024]{2,1,0:T(8,128)(2,1)S(1)}, bf16[9,16,1024]{2,1,0:T(8,128)(2,1)S(1)}, u32[]{:S(2)}, u32[]{:S(2)}) collective-permute-start(bf16[9,16,1024]{2,1,0:T(8,128)(2,1)S(1)} %get-tuple-element.122), channel_id=1, source_target_pairs={{0,16},{8,24},{16,0},{24,8},{1,17},{9,25},{17,1},{25,9},{2,18},{10... | collective-permute-start | bytes 884744 | tf_op jit(solution)/shard_map/ppermute | solution.py:561
  110.8 9.1 %collective-permute-start.20 = (bf16[2,32,1024]{2,1,0:T(8,128)(2,1)S(1)}, bf16[2,32,1024]{2,1,0:T(8,128)(2,1)S(1)}, u32[]{:S(2)}, u32[]{:S(2)}) collective-permute-start(bf16[2,32,1024]{2,1,0:T(8,128)(2,1)S(1)} %hold_stream.1.refs_11_), channel_id=1, source_target_pairs={{0,6},{1,7},{2,4},{3,5},{4,2},{5,3},{6,0},{7,1},{8,14},{9,15},{10,... | collective-permute-start | bytes 393224 | tf_op jit(solution)/shard_map/ppermute | solution.py:564
  114.7 46.8 %copy-start.9 = (s32[32,2]{0,1:T(2,128)S(1)}, s32[32,2]{0,1:T(2,128)}, u32[]{:S(2)}) copy-start(s32[32,2]{0,1:T(2,128)} %param.25) | copy-start | bytes 772
  114.7 46.8 %copy-start.10 = (f32[32,2]{0,1:T(2,128)S(1)}, f32[32,2]{0,1:T(2,128)}, u32[]{:S(2)}) copy-start(f32[32,2]{0,1:T(2,128)} %param.26) | copy-start | bytes 772
  120.1 10.0 %collective-permute-start.21 = (bf16[9,16,1024]{2,1,0:T(8,128)(2,1)S(1)}, bf16[9,16,1024]{2,1,0:T(8,128)(2,1)S(1)}, u32[]{:S(2)}, u32[]{:S(2)}) collective-permute-start(bf16[9,16,1024]{2,1,0:T(8,128)(2,1)S(1)} %get-tuple-element.129), channel_id=1, source_target_pairs={{0,8},{8,0},{16,24},{24,16},{1,9},{9,1},{17,25},{25,17},{2,10},{10... | collective-permute-start | bytes 884744 | tf_op jit(solution)/shard_map/ppermute | solution.py:558
  121.2 9.9 %collective-permute-start.22 = (bf16[9,16,1024]{2,1,0:T(8,128)(2,1)S(1)}, bf16[9,16,1024]{2,1,0:T(8,128)(2,1)S(1)}, u32[]{:S(2)}, u32[]{:S(2)}) collective-permute-start(bf16[9,16,1024]{2,1,0:T(8,128)(2,1)S(1)} %get-tuple-element.130), channel_id=1, source_target_pairs={{0,16},{8,24},{16,0},{24,8},{1,17},{9,25},{17,1},{25,9},{2,18},{10... | collective-permute-start | bytes 884744 | tf_op jit(solution)/shard_map/ppermute | solution.py:561
  122.7 13.7 %collective-permute-start.25 = (bf16[9,16,1024]{2,1,0:T(8,128)(2,1)S(1)}, bf16[9,16,1024]{2,1,0:T(8,128)(2,1)S(1)}, u32[]{:S(2)}, u32[]{:S(2)}) collective-permute-start(bf16[9,16,1024]{2,1,0:T(8,128)(2,1)S(1)} %get-tuple-element.135), channel_id=1, source_target_pairs={{0,8},{8,0},{16,24},{24,16},{1,9},{9,1},{17,25},{25,17},{2,10},{10... | collective-permute-start | bytes 884744 | tf_op jit(solution)/shard_map/ppermute | solution.py:558
  123.7 13.8 %collective-permute-start.26 = (bf16[9,16,1024]{2,1,0:T(8,128)(2,1)S(1)}, bf16[9,16,1024]{2,1,0:T(8,128)(2,1)S(1)}, u32[]{:S(2)}, u32[]{:S(2)}) collective-permute-start(bf16[9,16,1024]{2,1,0:T(8,128)(2,1)S(1)} %get-tuple-element.136), channel_id=1, source_target_pairs={{0,16},{8,24},{16,0},{24,8},{1,17},{9,25},{17,1},{25,9},{2,18},{10... | collective-permute-start | bytes 884744 | tf_op jit(solution)/shard_map/ppermute | solution.py:561
  131.3 11.4 %collective-permute-start.23 = (bf16[9,16,1024]{2,1,0:T(8,128)(2,1)S(1)}, bf16[9,16,1024]{2,1,0:T(8,128)(2,1)S(1)}, u32[]{:S(2)}, u32[]{:S(2)}) collective-permute-start(bf16[9,16,1024]{2,1,0:T(8,128)(2,1)S(1)} %get-tuple-element.133), channel_id=1, source_target_pairs={{0,8},{8,0},{16,24},{24,16},{1,9},{9,1},{17,25},{25,17},{2,10},{10... | collective-permute-start | bytes 884744 | tf_op jit(solution)/shard_map/ppermute | solution.py:558
  132.3 11.5 %collective-permute-start.24 = (bf16[9,16,1024]{2,1,0:T(8,128)(2,1)S(1)}, bf16[9,16,1024]{2,1,0:T(8,128)(2,1)S(1)}, u32[]{:S(2)}, u32[]{:S(2)}) collective-permute-start(bf16[9,16,1024]{2,1,0:T(8,128)(2,1)S(1)} %get-tuple-element.134), channel_id=1, source_target_pairs={{0,16},{8,24},{16,0},{24,8},{1,17},{9,25},{17,1},{25,9},{2,18},{10... | collective-permute-start | bytes 884744 | tf_op jit(solution)/shard_map/ppermute | solution.py:561
  133.8 12.6 %collective-permute-start.31 = (bf16[9,16,1024]{2,1,0:T(8,128)(2,1)S(1)}, bf16[9,16,1024]{2,1,0:T(8,128)(2,1)S(1)}, u32[]{:S(2)}, u32[]{:S(2)}) collective-permute-start(bf16[9,16,1024]{2,1,0:T(8,128)(2,1)S(1)} %get-tuple-element.141.refs_6_), channel_id=1, source_target_pairs={{0,6},{1,7},{2,4},{3,5},{4,2},{5,3},{6,0},{7,1},{8,14},{9,15},{10,... | collective-permute-start | bytes 884744 | tf_op jit(solution)/shard_map/ppermute | solution.py:564
  137.6 13.9 %collective-permute-start.29 = (bf16[9,16,1024]{2,1,0:T(8,128)(2,1)S(1)}, bf16[9,16,1024]{2,1,0:T(8,128)(2,1)S(1)}, u32[]{:S(2)}, u32[]{:S(2)}) collective-permute-start(bf16[9,16,1024]{2,1,0:T(8,128)(2,1)S(1)} %get-tuple-element.147), channel_id=1, source_target_pairs={{0,8},{8,0},{16,24},{24,16},{1,9},{9,1},{17,25},{25,17},{2,10},{10... | collective-permute-start | bytes 884744 | tf_op jit(solution)/shard_map/ppermute | solution.py:558
  138.7 12.8 %collective-permute-start.30 = (bf16[9,16,1024]{2,1,0:T(8,128)(2,1)S(1)}, bf16[9,16,1024]{2,1,0:T(8,128)(2,1)S(1)}, u32[]{:S(2)}, u32[]{:S(2)}) collective-permute-start(bf16[9,16,1024]{2,1,0:T(8,128)(2,1)S(1)} %get-tuple-element.148), channel_id=1, source_target_pairs={{0,16},{8,24},{16,0},{24,8},{1,17},{9,25},{17,1},{25,9},{2,18},{10... | collective-permute-start | bytes 884744 | tf_op jit(solution)/shard_map/ppermute | solution.py:561
  143.9 7.8 %collective-permute-start.27 = (bf16[9,16,1024]{2,1,0:T(8,128)(2,1)S(1)}, bf16[9,16,1024]{2,1,0:T(8,128)(2,1)S(1)}, u32[]{:S(2)}, u32[]{:S(2)}) collective-permute-start(bf16[9,16,1024]{2,1,0:T(8,128)(2,1)S(1)} %get-tuple-element.144), channel_id=1, source_target_pairs={{0,8},{8,0},{16,24},{24,16},{1,9},{9,1},{17,25},{25,17},{2,10},{10... | collective-permute-start | bytes 884744 | tf_op jit(solution)/shard_map/ppermute | solution.py:558
  145.0 6.8 %collective-permute-start.28 = (bf16[9,16,1024]{2,1,0:T(8,128)(2,1)S(1)}, bf16[9,16,1024]{2,1,0:T(8,128)(2,1)S(1)}, u32[]{:S(2)}, u32[]{:S(2)}) collective-permute-start(bf16[9,16,1024]{2,1,0:T(8,128)(2,1)S(1)} %get-tuple-element.145), channel_id=1, source_target_pairs={{0,16},{8,24},{16,0},{24,8},{1,17},{9,25},{17,1},{25,9},{2,18},{10... | collective-permute-start | bytes 884744 | tf_op jit(solution)/shard_map/ppermute | solution.py:561
  146.5 12.9 %collective-permute-start.33 = (bf16[9,16,1024]{2,1,0:T(8,128)(2,1)S(1)}, bf16[9,16,1024]{2,1,0:T(8,128)(2,1)S(1)}, u32[]{:S(2)}, u32[]{:S(2)}) collective-permute-start(bf16[9,16,1024]{2,1,0:T(8,128)(2,1)S(1)} %get-tuple-element.149), channel_id=1, source_target_pairs={{0,4},{1,5},{2,6},{3,7},{4,0},{5,1},{6,2},{7,3},{8,12},{9,13},{10,... | collective-permute-start | bytes 884744 | tf_op jit(solution)/shard_map/ppermute | solution.py:564
  151.7 7.7 %collective-permute-start.32 = (bf16[9,16,1024]{2,1,0:T(8,128)(2,1)S(1)}, bf16[9,16,1024]{2,1,0:T(8,128)(2,1)S(1)}, u32[]{:S(2)}, u32[]{:S(2)}) collective-permute-start(bf16[9,16,1024]{2,1,0:T(8,128)(2,1)S(1)} %finish_1.1), channel_id=1, source_target_pairs={{0,2},{1,3},{2,0},{3,1},{4,6},{5,7},{6,4},{7,5},{8,10},{9,11},{10,... | collective-permute-start | bytes 884744 | tf_op jit(solution)/shard_map/ppermute | solution.py:564
  159.4 2.1 %collective-permute-start.34 = (bf16[2,9,16,1024]{3,2,1,0:T(8,128)(2,1)S(1)}, bf16[2,9,16,1024]{3,2,1,0:T(8,128)(2,1)S(1)}, u32[]{:S(2)}, u32[]{:S(2)}) collective-permute-start(bf16[2,9,16,1024]{3,2,1,0:T(8,128)(2,1)S(1)} %second_kernel.1), channel_id=1, source_target_pairs={{0,1},{1,0},{2,3},{3,2},{4,5},{5,4},{6,7},{7,6},{8,9},{9,8},{10,11... | collective-permute-start | bytes 1769480 | tf_op jit(solution)/shard_map/ppermute | solution.py:564
